TPU v7x, 256 devices: a whole 4x4x8 slice. The times are simulated.
256 devices in a mesh: seq: 32 (over z, y_lo, core), qry: 8 (over x, y_hi).
Axes of the slice: x: 4, y: 4 (y_hi: 2, y_lo: 2; y = y_hi * 2 + y_lo), z: 8, core: 2. Of those that a mesh axis runs over, the one named last changes fastest.
Arguments:
- x_inner: bfloat16 [8, 32768, 2048], P('qry', 'seq'), may hold values from -6 to 6
- z_gate: bfloat16 [8, 32768, 2048], P('qry', 'seq'), may hold values from -6 to 6
- b_proj: bfloat16 [8, 32768, 128], P('qry', 'seq'), may hold values from -0.5 to 0.5
- c_proj: bfloat16 [8, 32768, 128], P('qry', 'seq'), may hold values from -0.5 to 0.5
- decays: float32 [8, 32, 32768], P('qry', None, 'seq'), may hold values from 0 to 1
- d_skip: float32 [32], replicated, may hold values from 0.5 to 2
- norm_gain: float32 [2048], replicated, may hold values from 0.1 to 1.9
- w_head: bfloat16 [2048, 128], replicated, may hold values from -0.125 to 0.125
- queries: bfloat16 [128, 32, 128], P('qry'), may hold values from -6 to 6
- valid_len: int32 [8, 256], P('qry', 'seq'), may hold values from 32 to 128, as said below
- pair_ids: int32 [128], replicated, may hold values from 0 to 2047
Outputs:
- maxsim_scores: float32 [8, 256, 128], P('qry', 'seq')
- paired_score: float32 [128], replicated
Inputs may be any that keep to these rules, and one draw needn't show every extreme that they name: `valid_len`: in every document at least one passage has all 128 tokens valid. `pair_ids`: passage index d * 256 + k.
All inputs are finite; a program needn't handle non-finite values.
Results may differ from a plain program's by a relative error of at most 0.002.
Values may be sent and summed in bfloat16 or wider, within the bound.
No kernel may reach another device: no remote copies, remote signals or barrier semaphores. Data moves between devices by JAX's collectives and lax.ppermute only.
A program may use at most 192 MiB of HBM per device.

v0:
```python
import functools

import jax
import jax.numpy as jnp
from jax import lax
from jax.experimental import pallas as pl
from jax.experimental.pallas import tpu as pltpu
from jax.sharding import Mesh
from jax.sharding import PartitionSpec as P

HEADS = 32
HEAD_DIM = 64
STATE = 128
SPAN = 128
TOKENS = 1024
SPANS = TOKENS // SPAN
INNER = HEADS * HEAD_DIM
PAIRS = HEADS // 2
WIDE = 512
CHUNKS = INNER // WIDE
HALF = STATE // 2
ROWS = HALF + 16
QTOK = 32
QTOT = 128
EMB = 128
BLOCK = 256
F32 = jnp.float32
BF16 = jnp.bfloat16
NT = (((1,), (1,)), ((), ()))


def dot(a, b):
    return jnp.dot(a, b, preferred_element_type=F32)


def dot_nt(a, b):
    return lax.dot_general(a, b, NT, preferred_element_type=F32)


def iota(shape, dim):
    return lax.broadcasted_iota(jnp.int32, shape, dim)


def ones_where(cond):
    return jnp.where(cond, 1.0, 0.0).astype(BF16)


def split2(v):
    high = v.astype(BF16)
    return high, (v - high.astype(F32)).astype(BF16)


def split3(v):
    high = v.astype(BF16)
    rest = v - high.astype(F32)
    mid = rest.astype(BF16)
    return high, mid, (rest - mid.astype(F32)).astype(BF16)


def head_selector(rows, first_head, columns):
    head = iota((rows, columns), 0) & (HEADS - 1)
    return ones_where(head == first_head + (iota((rows, columns), 1) >> 6))


def states_kernel(core_ref, dec_ref, b_ref, x_ref, keep_ref, send_ref, w_ref, bt_ref, d_ref):
    step = pl.program_id(0)

    @pl.when(step == 0)
    def _():
        row, col = iota((SPAN + 16, SPAN), 0), iota((SPAN + 16, SPAN), 1)
        after = ones_where((col > row) | (row >= SPAN))
        after = jnp.concatenate([after, after, after], axis=1)
        later = jnp.zeros((16, HEADS), F32)
        for c in reversed(range(SPANS)):
            rows = slice(c * SPAN, (c + 1) * SPAN)
            logs = jnp.concatenate(split3(jnp.log2(dec_ref[:, rows])), axis=1)
            sums = dot_nt(after, logs)
            high, low = split2(jnp.exp2(sums[:SPAN] + later[:1]))
            w_ref[rows, :] = jnp.concatenate([high, low], axis=1)
            later = later + sums[SPAN:]
            bt_ref[:, rows] = b_ref[rows, :].T
        high, low = split2(jnp.exp2(later))
        place = iota((16, HEADS), 0)
        zero = jnp.zeros((16, HEADS), F32)
        d_ref[...] = jnp.where(
            place == 0, high.astype(F32), jnp.where(place == 1, low.astype(F32), zero)
        ).astype(BF16)

    selector = head_selector(2 * HEADS, step * (WIDE // HEAD_DIM), WIDE)
    weighted = (x_ref[...].astype(F32) * dot(w_ref[...], selector)).astype(BF16)
    state = dot(bt_ref[...], weighted)
    decay = dot(d_ref[...], selector[:HEADS]).astype(BF16)
    lower = core_ref[0] == 0
    mine = jnp.where(lower, state[:HALF], state[HALF:]).astype(BF16)
    other = jnp.where(lower, state[HALF:], state[:HALF]).astype(BF16)
    for k in range(WIDE // 128):
        lanes = slice(k * 128, (k + 1) * 128)
        keep_ref[k, :HALF, :] = mine[:, lanes]
        keep_ref[k, HALF:, :] = decay[:, lanes]
        send_ref[k, :HALF, :] = other[:, lanes]
        send_ref[k, HALF:, :] = decay[:, lanes]


def local_kernel(
    dec_ref, b_ref, c_ref, x_ref, z_ref, skip_ref, y_ref, gate_ref, g_ref, carry_ref, prior_ref, e_ref
):
    step = pl.program_id(0)

    @pl.when(step == 0)
    def _():
        carry_ref[...] = jnp.zeros_like(carry_ref)
        prior_ref[...] = jnp.zeros_like(prior_ref)
        e_ref[...] = head_selector(2 * HEADS, 0, INNER)

    row, col = iota((SPAN, SPAN), 0), iota((SPAN, SPAN), 1)
    until = ones_where(col <= row)
    after = ones_where(col > row)
    sums_of = jnp.concatenate([until, after, jnp.ones((16, SPAN), BF16)], axis=0)
    sums_of = jnp.concatenate([sums_of, sums_of, sums_of], axis=1)
    logs = jnp.concatenate(split3(jnp.log2(dec_ref[...])), axis=1)
    sums = dot_nt(sums_of, logs)
    cum = sums[:SPAN]
    rows_until = ones_where(row <= col)
    cum_rows = dot(logs, jnp.concatenate([rows_until, rows_until, rows_until], axis=0))
    prior = prior_ref[...]
    prior_ref[...] = prior + sums[2 * SPAN : 2 * SPAN + 8]
    high, low = split2(jnp.exp2(cum + prior[:1]))
    g_ref[...] = jnp.concatenate([high, low], axis=1)
    factors = jnp.concatenate(split2(jnp.exp2(sums)), axis=1)
    c_span, b_span = c_ref[...], b_ref[...]
    b_turned = b_span.T
    cross = jnp.where(col <= row, dot_nt(c_span, b_span), 0.0)
    left = col < HEAD_DIM
    for j in range(CHUNKS):
        wide = slice(j * WIDE, (j + 1) * WIDE)
        spread_out = dot(factors, e_ref[:, wide])
        carry = carry_ref[:, wide]
        read = dot(c_span, carry.astype(BF16)) * spread_out[:SPAN]
        x_wide = x_ref[:, wide].astype(F32)
        parts = []
        for k in range(WIDE // 128):
            mixes = []
            for h in (j * 8 + 2 * k, j * 8 + 2 * k + 1):
                spread = jnp.minimum(cum[:, h : h + 1] - cum_rows[h : h + 1, :], 0.0)
                mixes.append((jnp.exp2(spread) * cross).astype(BF16))
            x_pair = x_ref[:, j * WIDE + k * 128 : j * WIDE + (k + 1) * 128]
            none = jnp.zeros_like(x_pair)
            x_both = jnp.concatenate(
                [jnp.where(left, x_pair, none), jnp.where(left, none, x_pair)], axis=0
            )
            parts.append(dot(jnp.concatenate(mixes, axis=1), x_both))
        y = jnp.concatenate(parts, axis=1) + read + skip_ref[:, wide] * x_wide
        y_ref[:, wide] = y.astype(BF16)
        weighted = (x_wide * spread_out[SPAN : 2 * SPAN]).astype(BF16)
        carry_ref[:, wide] = spread_out[2 * SPAN : 2 * SPAN + 1] * carry + dot(b_turned, weighted)
        z_half = 0.5 * z_ref[:, wide].astype(F32)
        gate_ref[:, wide] = (z_half + z_half * jnp.tanh(z_half)).astype(BF16)


def scan_kernel(in_ref, out_ref):
    carry = jnp.zeros((HALF, 128), F32)
    for k in range(PAIRS):
        out_ref[k] = carry.astype(BF16)
        decay = in_ref[k, HALF : HALF + 8, :].astype(F32)
        decay = decay[0:1] + decay[1:2]
        carry = decay * carry + in_ref[k, :HALF, :].astype(F32)


def score_kernel(
    base_ref, valid_ref, keep_ref, got_ref, c_ref, g_ref, y_ref, gate_ref, gain_ref, head_ref,
    q_ref, pair_ref, score_ref, paired_ref, e_ref, mean_ref, best_ref
):
    step = pl.program_id(0)

    @pl.when(step == 0)
    def _():
        e_ref[...] = head_selector(2 * HEADS, 0, INNER)
        same = (iota((256, 256), 0) >> 6) == (iota((256, 256), 1) >> 6)
        mean_ref[...] = jnp.where(same, 1.0 / HEAD_DIM, 0.0).astype(BF16)

    factors, c_part = g_ref[...], c_ref[...]
    embedded = jnp.zeros((BLOCK, EMB), F32)
    for j in range(CHUNKS):
        wide = slice(j * WIDE, (j + 1) * WIDE)
        entering = jnp.concatenate(
            [
                jnp.concatenate([keep_ref[4 * j + k], got_ref[4 * j + k]], axis=0)
                for k in range(WIDE // 128)
            ],
            axis=1,
        )
        y = y_ref[:, wide].astype(F32) + dot(factors, e_ref[:, wide]) * dot(c_part, entering)
        gated = y * gate_ref[:, wide].astype(F32)
        squares = (gated * gated).astype(BF16)
        means = jnp.concatenate(
            [dot(squares[:, k : k + 256], mean_ref[...]) for k in range(0, WIDE, 256)], axis=1
        )
        normed = (gated * lax.rsqrt(means + 1e-05) * gain_ref[:, wide]).astype(BF16)
        embedded = embedded + dot(normed, head_ref[wide, :])
    embedded = embedded * lax.rsqrt(jnp.sum(embedded * embedded, axis=1, keepdims=True) + 1e-06)
    for p in range(BLOCK // SPAN):
        passage = step * (BLOCK // SPAN) + p
        vectors = embedded[p * SPAN : (p + 1) * SPAN]
        kept = iota((SPAN, EMB), 0) < valid_ref[0, passage]
        vectors = jnp.where(kept, vectors, vectors[:1]).astype(BF16)
        for j in range(QTOK * QTOT // 1024):
            lanes = slice(j * 1024, (j + 1) * 1024)
            sims = dot_nt(vectors, q_ref[lanes, :])
            best_ref[pl.ds(passage, 1), lanes] = jnp.max(sims, axis=0, keepdims=True)

    @pl.when(step == TOKENS // BLOCK - 1)
    def _():
        total = best_ref[:, :QTOT]
        for i in range(1, QTOK):
            total = total + best_ref[:, i * QTOT : (i + 1) * QTOT]
        score_ref[...] = total
        matched = pair_ref[...] == base_ref[0] + iota((SPANS, QTOT), 0)
        paired = jnp.sum(jnp.where(matched, total, 0.0), axis=0, keepdims=True)
        paired_ref[...] = jnp.broadcast_to(paired, paired_ref.shape)


def whole(shape, space=None):
    kind = {} if space is None else {"memory_space": space}
    return pl.BlockSpec(shape, lambda i: (0,) * len(shape), **kind)


def params(mib):
    return pltpu.CompilerParams(
        dimension_semantics=("arbitrary",), vmem_limit_bytes=mib * 1024 * 1024
    )


def cost(flops, bytes_accessed, transcendentals=0):
    return pl.CostEstimate(
        flops=flops, bytes_accessed=bytes_accessed, transcendentals=transcendentals
    )


def device_states(core, decays, b, x):
    smem = pl.BlockSpec(memory_space=pltpu.SMEM)
    packed = jax.ShapeDtypeStruct((PAIRS, ROWS, 128), BF16)
    blocks = pl.BlockSpec((WIDE // 128, ROWS, 128), lambda i: (i, 0, 0))
    return pl.pallas_call(
        states_kernel,
        grid=(CHUNKS,),
        in_specs=[
            smem,
            whole((HEADS, TOKENS)),
            whole((TOKENS, STATE)),
            pl.BlockSpec((TOKENS, WIDE), lambda i: (0, i)),
        ],
        out_specs=[blocks, blocks],
        out_shape=[packed, packed],
        scratch_shapes=[
            pltpu.VMEM((TOKENS, 2 * HEADS), BF16),
            pltpu.VMEM((STATE, TOKENS), BF16),
            pltpu.VMEM((16, HEADS), BF16),
        ],
        compiler_params=params(20),
        cost_estimate=cost(10**9, 5 * 10**6),
        name="device_states",
    )(core, decays, b, x)


def local_part(decays, b, c, x, z, skip):
    def tokens(width):
        return pl.BlockSpec((SPAN, width), lambda i: (i, 0))

    return pl.pallas_call(
        local_kernel,
        grid=(SPANS,),
        in_specs=[
            pl.BlockSpec((HEADS, SPAN), lambda i: (0, i)),
            tokens(STATE),
            tokens(STATE),
            tokens(INNER),
            tokens(INNER),
            whole((1, INNER)),
        ],
        out_specs=[tokens(INNER), tokens(INNER), tokens(2 * HEADS)],
        out_shape=[
            jax.ShapeDtypeStruct((TOKENS, INNER), BF16),
            jax.ShapeDtypeStruct((TOKENS, INNER), BF16),
            jax.ShapeDtypeStruct((TOKENS, 2 * HEADS), BF16),
        ],
        scratch_shapes=[
            pltpu.VMEM((STATE, INNER), F32),
            pltpu.VMEM((8, HEADS), F32),
            pltpu.VMEM((2 * HEADS, INNER), BF16),
        ],
        compiler_params=params(20),
        cost_estimate=cost(8 * 10**9, 17 * 10**6, 6 * 10**6),
        name="local_part",
    )(decays, b, c, x, z, skip)


def scan_chips(states):
    return pl.pallas_call(
        scan_kernel,
        out_shape=jax.ShapeDtypeStruct((PAIRS, HALF, 128), BF16),
        cost_estimate=cost(10**6, 600_000),
        name="scan_chips",
    )(states)


def scores(base, valid_len, keep, got, c, growth, y, gate, gain, w_head, q, pair_ids):
    def tokens(width):
        return pl.BlockSpec((BLOCK, width), lambda i: (i, 0))

    smem = pl.BlockSpec(memory_space=pltpu.SMEM)
    half = whole((PAIRS, HALF, 128))
    everyone = 256
    return pl.pallas_call(
        score_kernel,
        grid=(TOKENS // BLOCK,),
        in_specs=[
            smem,
            smem,
            half,
            half,
            tokens(STATE),
            tokens(2 * HEADS),
            tokens(INNER),
            tokens(INNER),
            whole((1, INNER)),
            whole((INNER, EMB)),
            whole((QTOK * QTOT, EMB)),
            whole((1, QTOT)),
        ],
        out_specs=[whole((SPANS, QTOT)), whole((everyone, QTOT))],
        out_shape=[
            jax.ShapeDtypeStruct((SPANS, QTOT), F32),
            jax.ShapeDtypeStruct((everyone, QTOT), F32),
        ],
        scratch_shapes=[
            pltpu.VMEM((2 * HEADS, INNER), BF16),
            pltpu.VMEM((256, 256), BF16),
            pltpu.VMEM((SPANS, QTOK * QTOT), F32),
        ],
        compiler_params=params(24),
        cost_estimate=cost(6 * 10**9, 11 * 10**6, 2 * 10**6),
        name="scores",
    )(base, valid_len, keep, got, c, growth, y, gate, gain, w_head, q, pair_ids)


def swap_cores(v):
    return lax.ppermute(v, "core", [(0, 1), (1, 0)])


def decay_of(packed):
    return packed[:, HALF : HALF + 1].astype(F32) + packed[:, HALF + 1 : HALF + 2].astype(F32)


def on_device(
    x_inner, z_gate, b_proj, c_proj, decays, d_skip, norm_gain, w_head, queries, valid_len, pair_ids
):
    core = lax.axis_index("core")
    x, z, b, c, decay = x_inner[0], z_gate[0], b_proj[0], c_proj[0], decays[0]

    wide = queries.astype(F32)
    q = (wide * lax.rsqrt(jnp.sum(wide * wide, axis=-1, keepdims=True) + 1e-06)).astype(BF16)
    q = jnp.broadcast_to(q.transpose(1, 0, 2)[None], (8, QTOK, 16, EMB))
    q = lax.all_to_all(q, ("x", "y_hi"), 0, 0, tiled=True)
    q = q.transpose(1, 0, 2, 3).reshape(QTOK * QTOT, EMB)

    own, send = device_states(core.reshape(1), decay, b, x)
    got = swap_cores(send)
    lower = core == 0
    first = jnp.where(lower, own, got)
    second = jnp.where(lower, got, own)
    d_first, d_second = decay_of(first), decay_of(second)
    chip = d_second * first[:, :HALF].astype(F32) + second[:, :HALF].astype(F32)
    high, low = split2(d_first * d_second)
    fill = jnp.zeros((PAIRS, 14, 128), BF16)
    packed = jnp.concatenate([chip.astype(BF16), high, low, fill], axis=1)
    by_pair = lax.all_to_all(packed, ("z", "y_lo"), 0, 0, tiled=True)

    y_local, gate, growth = local_part(
        decay, b, c, x, z, jnp.repeat(d_skip, HEAD_DIM).reshape(1, INNER)
    )

    entering = lax.all_to_all(scan_chips(by_pair), ("z", "y_lo"), 0, 0, tiled=True)
    after = (
        d_first * entering.astype(F32) + first[:, :HALF].astype(F32)
    ).astype(BF16)
    keep = jnp.where(lower, entering, after)
    got = swap_cores(jnp.where(lower, after, entering))
    c_turned = jnp.where(lower, c, jnp.roll(c, HALF, axis=1))

    document = lax.axis_index(("x", "y_hi"))
    place = lax.axis_index(("z", "y_lo", "core"))
    base = (document * 32 + place) * SPANS
    maxsim, paired = scores(
        base.reshape(1), valid_len, keep, got, c_turned, growth, y_local, gate,
        norm_gain.reshape(1, INNER), w_head, q, pair_ids.reshape(1, QTOT),
    )
    everything = lax.all_to_all(paired, ("z", "y_lo", "core", "x", "y_hi"), 0, 0, tiled=True)
    return maxsim[None], jnp.sum(everything, axis=0)


def solution(mesh):
    cut = Mesh(mesh.devices.reshape(8, 2, 2, 4, 2), ("z", "y_lo", "core", "x", "y_hi"))
    seq, qry = ("z", "y_lo", "core"), ("x", "y_hi")
    return jax.shard_map(
        on_device,
        mesh=cut,
        in_specs=(
            P(qry, seq, None),
            P(qry, seq, None),
            P(qry, seq, None),
            P(qry, seq, None),
            P(qry, None, seq),
            P(),
            P(),
            P(),
            P(qry, None, None),
            P(qry, seq),
            P(),
        ),
        out_specs=(P(qry, seq, None), P()),
        check_vma=False,
    )
```

profile of v0, /device:TPU:1, one launch (start us, length us, event | category | flops | bytes accessed | tf_op | source)
XLA Modules:
  0.0 121.7 jit_solution(18353645734761730671)
XLA Ops:
  0.6 2.2 %copy-done = bf16[1,1024,2048]{2,1,0:T(8,128)(2,1)S(1)} copy-done((bf16[1,1024,2048]{2,1,0:T(8,128)(2,1)S(1)}, bf16[1,1024,2048]{2,1,0:T(8,128)(2,1)}, u32[]{:S(2)}) %copy-start) | copy-done | bytes 4194328
  2.8 0.9 copy-done.3
  3.8 0.9 copy-done.5
  4.7 3.2 %device_states.1 = (bf16[16,80,128]{2,1,0:T(8,128)(2,1)S(1)}, bf16[16,80,128]{2,1,0:T(8,128)(2,1)S(1)}) custom-call(s32[1]{0:T(128)} %bitcast.1.core_ref, f32[32,1024]{1,0:T(8,128)S(1)} %bitcast.27, bf16[1024,128]{1,0:T(8,128)(2,1)S(1)} %bitcast.25, bf16[1024,2048]{1,0:T(8,128)(2,1)S(1)} %bitcast.20), custom_call_target="tpu_custom_call" | custom-call | flops 1000000000 | bytes 5000000 | tf_op jit(solution)/shard_map/device_states/pallas_call | solution.py:243
  7.9 3.3 %collective-permute-start = (bf16[16,80,128]{2,1,0:T(8,128)(2,1)S(1)}, bf16[16,80,128]{2,1,0:T(8,128)(2,1)S(1)}, u32[]{:S(2)}, u32[]{:S(2)}) collective-permute-start(bf16[16,80,128]{2,1,0:T(8,128)(2,1)S(1)} %get-tuple-element.9), channel_id=1, source_target_pairs={{0,8},{8,0},{1,9},{9,1},{2,10},{10,2},{3,11},{11,3},{4,12},{12,4},... | collective-permute-start | bytes 983048 | tf_op jit(solution)/shard_map/ppermute | solution.py:347
  11.3 1.2 collective-permute-done
  12.6 0.1 fusion.1
  12.7 0.1 maximum_maximum_fusion
  12.9 19.8 %all_to_all.24.in_ref = bf16[16,80,128]{2,1,0:T(8,128)(2,1)} all-to-all(bf16[16,80,128]{2,1,0:T(8,128)(2,1)S(1)} %maximum_maximum_fusion), channel_id=1, replica_groups=mesh['z'=8,'y_lo'=2,'core'=2,'x'=4,'y_hi'=2] {'z','y_lo'}, dimensions={0} | all-to-all | bytes 655360 | tf_op jit(solution)/shard_map/all_to_all | solution.py:376
  32.7 1.7 %scan_chips.1 = bf16[16,64,128]{2,1,0:T(8,128)(2,1)} custom-call(bf16[16,80,128]{2,1,0:T(8,128)(2,1)} %all_to_all.24.in_ref), custom_call_target="tpu_custom_call" | custom-call | flops 1000000 | bytes 600000 | tf_op jit(solution)/shard_map/scan_chips/pallas_call | solution.py:298
  34.4 3.8 %all-to-all-start.1 = ((bf16[16,64,128]{2,1,0:T(8,128)(2,1)}), bf16[16,64,128]{2,1,0:T(8,128)(2,1)S(1)}, u32[]{:S(2)}, u32[]{:S(2)}) async-start(bf16[16,64,128]{2,1,0:T(8,128)(2,1)} %scan_chips.1), calls=%async_computation.1 | async-start | bytes 524288 | tf_op jit(solution)/shard_map/all_to_all | solution.py:382
  38.3 0.1 fusion.5
  38.6 0.1 fusion.7
  38.8 9.4 %all-to-all-done.1 = bf16[16,64,128]{2,1,0:T(8,128)(2,1)S(1)} async-done(((bf16[16,64,128]{2,1,0:T(8,128)(2,1)}), bf16[16,64,128]{2,1,0:T(8,128)(2,1)S(1)}, u32[]{:S(2)}, u32[]{:S(2)}) %all-to-all-start.1) | async-done | bytes 262176 | tf_op jit(solution)/shard_map/all_to_all | solution.py:382
  48.2 1.2 broadcast_in_dim.18
  49.4 6.4 %all-to-all-start.2 = ((bf16[8,32,16,128]{3,2,1,0:T(8,128)(2,1)}), bf16[8,32,16,128]{3,2,1,0:T(8,128)(2,1)S(1)}, u32[]{:S(2)}, u32[]{:S(2)}) async-start(bf16[8,32,16,128]{3,2,1,0:T(8,128)(2,1)} %broadcast_in_dim.18), calls=%async_computation.2 | async-start | bytes 2097152 | tf_op jit(solution)/shard_map/all_to_all | solution.py:363
  55.8 2.2 %copy-done.1 = bf16[1,1024,2048]{2,1,0:T(8,128)(2,1)S(1)} copy-done((bf16[1,1024,2048]{2,1,0:T(8,128)(2,1)S(1)}, bf16[1,1024,2048]{2,1,0:T(8,128)(2,1)}, u32[]{:S(2)}) %copy-start.1) | copy-done | bytes 4194328
  58.0 2.2 %copy-done.7 = bf16[1,1024,2048]{2,1,0:T(8,128)(2,1)S(1)} copy-done((bf16[1,1024,2048]{2,1,0:T(8,128)(2,1)S(1)}, bf16[1,1024,2048]{2,1,0:T(8,128)(2,1)}, u32[]{:S(2)}) %copy-start.7) | copy-done | bytes 4194328
  60.2 13.5 %local_part.1 = (bf16[1024,2048]{1,0:T(8,128)(2,1)S(1)}, bf16[1024,2048]{1,0:T(8,128)(2,1)S(1)}, bf16[1024,64]{1,0:T(8,128)(2,1)S(1)}) custom-call(f32[32,1024]{1,0:T(8,128)S(1)} %bitcast.28, bf16[1024,128]{1,0:T(8,128)(2,1)S(1)} %bitcast.26, bf16[1024,128]{1,0:T(8,128)(2,1)S(1)} %bitcast.22, bf16[1024,2048]{1,0:T(8,128)(2,1)S(1)} %bitcast.21, ...), custom_call_target="tpu_custom_call" | custom-call | flops 8000000000 | bytes 17000000 | tf_op jit(solution)/shard_map/local_part/pallas_call | solution.py:269
  73.7 1.9 %copy-done.12 = bf16[1024,2048]{1,0:T(8,128)(2,1)} copy-done((bf16[1024,2048]{1,0:T(8,128)(2,1)}, bf16[1024,2048]{1,0:T(8,128)(2,1)S(1)}, u32[]{:S(2)}) %copy-start.12) | copy-done | bytes 4194328
  75.6 2.0 %copy-done.14 = bf16[1024,2048]{1,0:T(8,128)(2,1)} copy-done((bf16[1024,2048]{1,0:T(8,128)(2,1)}, bf16[1024,2048]{1,0:T(8,128)(2,1)S(1)}, u32[]{:S(2)}) %copy-start.14) | copy-done | bytes 4194328
  77.7 0.9 fusion.3
  78.5 3.5 %collective-permute-start.1 = (bf16[16,64,128]{2,1,0:T(8,128)(2,1)}, bf16[16,64,128]{2,1,0:T(8,128)(2,1)S(1)}, u32[]{:S(2)}, u32[]{:S(2)}) collective-permute-start(bf16[16,64,128]{2,1,0:T(8,128)(2,1)} %get-tuple-element.21), channel_id=1, source_target_pairs={{0,8},{8,0},{1,9},{9,1},{2,10},{10,2},{3,11},{11,3},{4,12},{12,4},... | collective-permute-start | bytes 786440 | tf_op jit(solution)/shard_map/ppermute | solution.py:347
  82.0 0.1 fusion.12
  82.1 0.2 maximum_select_fusion.c_ref
  82.3 0.3 copy.15
  82.6 0.7 collective-permute-done.1.got_ref
  83.4 2.2 %copy-done.13 = bf16[1024,2048]{1,0:T(8,128)(2,1)S(1)} copy-done((bf16[1024,2048]{1,0:T(8,128)(2,1)S(1)}, bf16[1024,2048]{1,0:T(8,128)(2,1)}, u32[]{:S(2)}) %copy-start.13) | copy-done | bytes 4194328
  85.6 2.2 %copy-done.15 = bf16[1024,2048]{1,0:T(8,128)(2,1)S(1)} copy-done((bf16[1024,2048]{1,0:T(8,128)(2,1)S(1)}, bf16[1024,2048]{1,0:T(8,128)(2,1)}, u32[]{:S(2)}) %copy-start.15) | copy-done | bytes 4194328
  87.8 11.5 %scores.1 = (f32[8,128]{1,0:T(8,128)}, f32[256,128]{1,0:T(8,128)S(1)}) custom-call(s32[1]{0:T(128)} %bitcast.base_ref, s32[1,8]{1,0:T(1,128)S(1)} %copy-done.10, bf16[16,64,128]{2,1,0:T(8,128)(2,1)S(1)} %get-tuple-element.22.keep_ref, bf16[16,64,128]{2,1,0:T(8,128)(2,1)S(1)} %collective-permute-done.1.got_ref, ...), custom_call_target="tpu_custom_call" | custom-call | flops 6000000000 | bytes 11000000 | tf_op jit(solution)/shard_map/scores/pallas_call | solution.py:313
  99.3 21.6 %all_to_all.25 = f32[256,1,128]{2,1,0:T(1,128)S(1)} all-to-all(f32[256,1,128]{2,1,0:T(1,128)S(1)} %bitcast.29), channel_id=1, replica_groups=mesh['z'=8,'y_lo'=2,'core'=2,'x'=4,'y_hi'=2] {'z','y_lo','core','x','y_hi'}, dimensions={0} | all-to-all | bytes 262144 | tf_op jit(solution)/shard_map/all_to_all | solution.py:397
  120.9 0.8 reduce_sum.19
  (37 shorter events, 0.4 us)
Async XLA Ops:
  0.6 2.2 %copy-start = (bf16[1,1024,2048]{2,1,0:T(8,128)(2,1)S(1)}, bf16[1,1024,2048]{2,1,0:T(8,128)(2,1)}, u32[]{:S(2)}) copy-start(bf16[1,1024,2048]{2,1,0:T(8,128)(2,1)} %param.11) | copy-start | bytes 12582916
  2.8 0.9 copy-start.3
  3.8 0.9 copy-start.5
  4.7 33.6 %copy-start.16 = (bf16[16,32,128]{2,1,0:T(8,128)(2,1)S(1)}, bf16[16,32,128]{2,1,0:T(8,128)(2,1)}, u32[]{:S(2)}) copy-start(bf16[16,32,128]{2,1,0:T(8,128)(2,1)} %param.19) | copy-start | bytes 393220
  4.7 33.7 %copy-start.17 = (f32[32]{0:T(128)S(1)}, f32[32]{0:T(128)}, u32[]{:S(2)}) copy-start(f32[32]{0:T(128)} %param.16) | copy-start | bytes 388
  7.9 4.6 %collective-permute-start = (bf16[16,80,128]{2,1,0:T(8,128)(2,1)S(1)}, bf16[16,80,128]{2,1,0:T(8,128)(2,1)S(1)}, u32[]{:S(2)}, u32[]{:S(2)}) collective-permute-start(bf16[16,80,128]{2,1,0:T(8,128)(2,1)S(1)} %get-tuple-element.9), channel_id=1, source_target_pairs={{0,8},{8,0},{1,9},{9,1},{2,10},{10,2},{3,11},{11,3},{4,12},{12,4},... | collective-permute-start | bytes 983048 | tf_op jit(solution)/shard_map/ppermute | solution.py:347
  12.5 43.3 %copy-start.2 = (bf16[1,1024,128]{2,1,0:T(8,128)(2,1)S(1)}, bf16[1,1024,128]{2,1,0:T(8,128)(2,1)}, u32[]{:S(2)}) copy-start(bf16[1,1024,128]{2,1,0:T(8,128)(2,1)} %param.14) | copy-start | bytes 786436
  12.5 43.3 %copy-start.4 = (bf16[1,1024,128]{2,1,0:T(8,128)(2,1)S(1)}, bf16[1,1024,128]{2,1,0:T(8,128)(2,1)}, u32[]{:S(2)}) copy-start(bf16[1,1024,128]{2,1,0:T(8,128)(2,1)} %param.13) | copy-start | bytes 786436
  12.5 43.3 %copy-start.6 = (f32[1,32,1024]{2,1,0:T(8,128)S(1)}, f32[1,32,1024]{2,1,0:T(8,128)}, u32[]{:S(2)}) copy-start(f32[1,32,1024]{2,1,0:T(8,128)} %param.15) | copy-start | bytes 393220
  34.4 13.8 %all-to-all-start.1 = ((bf16[16,64,128]{2,1,0:T(8,128)(2,1)}), bf16[16,64,128]{2,1,0:T(8,128)(2,1)S(1)}, u32[]{:S(2)}, u32[]{:S(2)}) async-start(bf16[16,64,128]{2,1,0:T(8,128)(2,1)} %scan_chips.1), calls=%async_computation.1 | async-start | bytes 524288 | tf_op jit(solution)/shard_map/all_to_all | solution.py:382
  49.4 32.9 %all-to-all-start.2 = ((bf16[8,32,16,128]{3,2,1,0:T(8,128)(2,1)}), bf16[8,32,16,128]{3,2,1,0:T(8,128)(2,1)S(1)}, u32[]{:S(2)}, u32[]{:S(2)}) async-start(bf16[8,32,16,128]{3,2,1,0:T(8,128)(2,1)} %broadcast_in_dim.18), calls=%async_computation.2 | async-start | bytes 2097152 | tf_op jit(solution)/shard_map/all_to_all | solution.py:363
  55.8 2.2 %copy-start.1 = (bf16[1,1024,2048]{2,1,0:T(8,128)(2,1)S(1)}, bf16[1,1024,2048]{2,1,0:T(8,128)(2,1)}, u32[]{:S(2)}) copy-start(bf16[1,1024,2048]{2,1,0:T(8,128)(2,1)} %param.11) | copy-start | bytes 12582916
  58.0 2.2 %copy-start.7 = (bf16[1,1024,2048]{2,1,0:T(8,128)(2,1)S(1)}, bf16[1,1024,2048]{2,1,0:T(8,128)(2,1)}, u32[]{:S(2)}) copy-start(bf16[1,1024,2048]{2,1,0:T(8,128)(2,1)} %param.12) | copy-start | bytes 12582916
  73.7 1.9 %copy-start.12 = (bf16[1024,2048]{1,0:T(8,128)(2,1)}, bf16[1024,2048]{1,0:T(8,128)(2,1)S(1)}, u32[]{:S(2)}) copy-start(bf16[1024,2048]{1,0:T(8,128)(2,1)S(1)} %get-tuple-element.12.y_ref) | copy-start | bytes 12582916
  75.6 2.0 %copy-start.14 = (bf16[1024,2048]{1,0:T(8,128)(2,1)}, bf16[1024,2048]{1,0:T(8,128)(2,1)S(1)}, u32[]{:S(2)}) copy-start(bf16[1024,2048]{1,0:T(8,128)(2,1)S(1)} %get-tuple-element.13.gate_ref) | copy-start | bytes 12582916
  77.6 5.7 %copy-start.8 = (bf16[2048,128]{1,0:T(8,128)(2,1)S(1)}, bf16[2048,128]{1,0:T(8,128)(2,1)}, u32[]{:S(2)}) copy-start(bf16[2048,128]{1,0:T(8,128)(2,1)} %head_ref.1) | copy-start | bytes 1572868
  77.6 5.7 %copy-start.9 = (f32[2048]{0:T(1024)S(1)}, f32[2048]{0:T(1024)}, u32[]{:S(2)}) copy-start(f32[2048]{0:T(1024)} %param.17) | copy-start | bytes 24580
  77.6 5.7 %copy-start.10 = (s32[1,8]{1,0:T(1,128)S(1)}, s32[1,8]{1,0:T(1,128)}, u32[]{:S(2)}) copy-start(s32[1,8]{1,0:T(1,128)} %valid_ref.1) | copy-start | bytes 100
  77.6 5.7 %copy-start.11 = (s32[128]{0:T(128)S(1)}, s32[128]{0:T(128)}, u32[]{:S(2)}) copy-start(s32[128]{0:T(128)} %param.21) | copy-start | bytes 1540
  78.5 4.8 %collective-permute-start.1 = (bf16[16,64,128]{2,1,0:T(8,128)(2,1)}, bf16[16,64,128]{2,1,0:T(8,128)(2,1)S(1)}, u32[]{:S(2)}, u32[]{:S(2)}) collective-permute-start(bf16[16,64,128]{2,1,0:T(8,128)(2,1)} %get-tuple-element.21), channel_id=1, source_target_pairs={{0,8},{8,0},{1,9},{9,1},{2,10},{10,2},{3,11},{11,3},{4,12},{12,4},... | collective-permute-start | bytes 786440 | tf_op jit(solution)/shard_map/ppermute | solution.py:347
  83.4 2.2 %copy-start.13 = (bf16[1024,2048]{1,0:T(8,128)(2,1)S(1)}, bf16[1024,2048]{1,0:T(8,128)(2,1)}, u32[]{:S(2)}) copy-start(bf16[1024,2048]{1,0:T(8,128)(2,1)} %copy-done.12) | copy-start | bytes 12582916
  85.6 2.2 %copy-start.15 = (bf16[1024,2048]{1,0:T(8,128)(2,1)S(1)}, bf16[1024,2048]{1,0:T(8,128)(2,1)}, u32[]{:S(2)}) copy-start(bf16[1024,2048]{1,0:T(8,128)(2,1)} %copy-done.14) | copy-start | bytes 12582916
where the time goes:
time: 122 us
  blocking collectives  41.4 us (34%)
  Pallas kernels  30 us (25%)
  local copies, waits for them, and re-layouts  18.7 us (15%)
  starting transfers between devices  17 us (14%)
  waiting for transfers between devices  11.3 us (9%)
  other arithmetic  2.44 us (2%)
    all_to_all x1, blocking collectives, on_device(): lax.all_to_all(paired, ('z', 'y_lo', 'core', 'x', 'y_hi'), 0, 0, tiled=True)  21.6 us
    all_to_all x1, blocking collectives, on_device(): by_pair = lax.all_to_all(packed, ('z', 'y_lo'), 0, 0, tiled=True)  19.8 us
    unnamed x36, local copies, waits for them, and re-layouts  16.8 us
    pallas_call x1, Pallas kernels, local_part(): pl.pallas_call(local_kernel, grid=(SPANS,), in_specs=[pl.BlockSpec((HEADS...  13.5 us
    pallas_call x1, Pallas kernels, scores(): pl.pallas_call(score_kernel, grid=(TOKENS // BLOCK,), in_specs=[smem, sme...  11.5 us
    all_to_all x1, waiting for transfers between devices, on_device(): lax.all_to_all(scan_chips(by_pair), ('z', 'y_lo'), 0, 0, tiled=True)  9.39 us
    ppermute x2, starting transfers between devices, swap_cores(): return lax.ppermute(v, 'core', [(0, 1), (1, 0)])  6.79 us
    all_to_all x1, starting transfers between devices, on_device(): q = lax.all_to_all(q, ('x', 'y_hi'), 0, 0, tiled=True)  6.36 us
  transfers between devices with their start and end apart: 4, of which 3 were waited for; matrix products, arithmetic and copies ran while one was open for 2% of the time, Pallas kernels for 11%

commit v1 on v0

v1 whole, which is shorter than its diff:
```python
import functools

import jax
import jax.numpy as jnp
from jax import lax
from jax.experimental import pallas as pl
from jax.experimental.pallas import tpu as pltpu
from jax.sharding import Mesh
from jax.sharding import PartitionSpec as P

HEADS = 32
HEAD_DIM = 64
STATE = 128
SPAN = 128
TOKENS = 1024
SPANS = TOKENS // SPAN
INNER = HEADS * HEAD_DIM
PAIRS = HEADS // 2
WIDE = 512
CHUNKS = INNER // WIDE
HALF = STATE // 2
ROWS = HALF + 16
QTOK = 32
QTOT = 128
EMB = 128
BLOCK = 256
TOGETHER = 2
F32 = jnp.float32
BF16 = jnp.bfloat16
NT = (((1,), (1,)), ((), ()))


def dot(a, b):
    return jnp.dot(a, b, preferred_element_type=F32)


def dot_nt(a, b):
    return lax.dot_general(a, b, NT, preferred_element_type=F32)


def iota(shape, dim):
    return lax.broadcasted_iota(jnp.int32, shape, dim)


def ones_where(cond):
    return jnp.where(cond, 1.0, 0.0).astype(BF16)


def split2(v):
    high = v.astype(BF16)
    return high, (v - high.astype(F32)).astype(BF16)


def split3(v):
    high = v.astype(BF16)
    rest = v - high.astype(F32)
    mid = rest.astype(BF16)
    return high, mid, (rest - mid.astype(F32)).astype(BF16)


def head_selector(rows, first_head, columns):
    head = iota((rows, columns), 0) & (HEADS - 1)
    return ones_where(head == first_head + (iota((rows, columns), 1) >> 6))


def states_kernel(
    core_ref, dec_any, b_any, x_any, keep_ref, send_ref, dec_ref, b_ref, x_ref, w_ref, bt_ref, sems
):
    get_dec = pltpu.make_async_copy(dec_any, dec_ref, sems.at[CHUNKS])
    get_b = pltpu.make_async_copy(b_any, b_ref, sems.at[CHUNKS + 1])
    get_x = [
        pltpu.make_async_copy(x_any.at[:, j * WIDE : (j + 1) * WIDE], x_ref.at[j], sems.at[j])
        for j in range(CHUNKS)
    ]
    for copy in (get_dec, get_b, *get_x):
        copy.start()
    row, col = iota((SPAN + 16, SPAN), 0), iota((SPAN + 16, SPAN), 1)
    after = ones_where((col > row) | (row >= SPAN))
    after = jnp.concatenate([after, after, after], axis=1)
    get_dec.wait()
    sums = [
        dot_nt(
            after,
            jnp.concatenate(
                split3(jnp.log2(dec_ref[:, c * SPAN : (c + 1) * SPAN])), axis=1
            ),
        )
        for c in range(SPANS)
    ]
    later = jnp.zeros((16, HEADS), F32)
    for c in reversed(range(SPANS)):
        high, low = split2(jnp.exp2(sums[c][:SPAN] + later[:1]))
        w_ref[c * SPAN : (c + 1) * SPAN, :] = jnp.concatenate([high, low], axis=1)
        later = later + sums[c][SPAN:]
    high, low = split2(jnp.exp2(later))
    place = iota((16, HEADS), 0)
    zero = jnp.zeros((16, HEADS), F32)
    decays = jnp.where(
        place == 0, high.astype(F32), jnp.where(place == 1, low.astype(F32), zero)
    ).astype(BF16)
    get_b.wait()
    for c in range(SPANS):
        rows = slice(c * SPAN, (c + 1) * SPAN)
        bt_ref[:, rows] = b_ref[rows, :].T
    lower = core_ref[0] == 0
    for j in range(CHUNKS):
        selector = head_selector(2 * HEADS, j * (WIDE // HEAD_DIM), WIDE)
        decay = dot(decays, selector[:HEADS]).astype(BF16)
        spread_out = dot(w_ref[...], selector)
        get_x[j].wait()
        weighted = (x_ref[j].astype(F32) * spread_out).astype(BF16)
        state = dot(bt_ref[...], weighted)
        mine = jnp.where(lower, state[:HALF], state[HALF:]).astype(BF16)
        other = jnp.where(lower, state[HALF:], state[:HALF]).astype(BF16)
        for k in range(WIDE // 128):
            lanes = slice(k * 128, (k + 1) * 128)
            pair = j * (WIDE // 128) + k
            keep_ref[pair, :HALF, :] = mine[:, lanes]
            keep_ref[pair, HALF:, :] = decay[:, lanes]
            send_ref[pair, :HALF, :] = other[:, lanes]
            send_ref[pair, HALF:, :] = decay[:, lanes]


def local_kernel(
    dec_ref, b_ref, c_ref, x_ref, skip_ref, y_ref, g_ref,
    carry_ref, e_ref, cum_ref, rows_ref, factor_ref
):
    step = pl.program_id(0)
    row, col = iota((SPAN, SPAN), 0), iota((SPAN, SPAN), 1)

    @pl.when(step == 0)
    def _():
        carry_ref[...] = jnp.zeros_like(carry_ref)
        e_ref[...] = head_selector(2 * HEADS, 0, INNER)
        until = ones_where(col <= row)
        after = ones_where(col > row)
        sums_of = jnp.concatenate([until, after, jnp.ones((16, SPAN), BF16)], axis=0)
        sums_of = jnp.concatenate([sums_of, sums_of, sums_of], axis=1)
        rows_until = ones_where(row <= col)
        rows_until = jnp.concatenate([rows_until, rows_until, rows_until], axis=0)
        prior = jnp.zeros((1, HEADS), F32)
        for c in range(SPANS):
            logs = jnp.log2(dec_ref[:, c * SPAN : (c + 1) * SPAN])
            logs = jnp.concatenate(split3(logs), axis=1)
            sums = dot_nt(sums_of, logs)
            cum_ref[c] = sums[:SPAN]
            rows_ref[c] = dot(logs, rows_until)
            high, low = split2(jnp.exp2(sums[:SPAN] + prior))
            g_ref[c * SPAN : (c + 1) * SPAN, :] = jnp.concatenate([high, low], axis=1)
            prior = prior + sums[2 * SPAN : 2 * SPAN + 1]
            factor_ref[c] = jnp.concatenate(split2(jnp.exp2(sums)), axis=1)

    left = col < HEAD_DIM
    for u in range(TOGETHER):
        span = step * TOGETHER + u
        here = slice(u * SPAN, (u + 1) * SPAN)
        cum, cum_rows, factors = cum_ref[span], rows_ref[span], factor_ref[span]
        c_span, b_span = c_ref[here, :], b_ref[here, :]
        b_turned = b_span.T
        cross = jnp.where(col <= row, dot_nt(c_span, b_span), 0.0)
        for j in range(CHUNKS):
            wide = slice(j * WIDE, (j + 1) * WIDE)
            spread_out = dot(factors, e_ref[:, wide])
            carry = carry_ref[:, wide]
            read = dot(c_span, carry.astype(BF16)) * spread_out[:SPAN]
            x_wide = x_ref[here, wide].astype(F32)
            parts = []
            for k in range(WIDE // 128):
                mixes = []
                for h in (j * 8 + 2 * k, j * 8 + 2 * k + 1):
                    spread = jnp.minimum(cum[:, h : h + 1] - cum_rows[h : h + 1, :], 0.0)
                    mixes.append((jnp.exp2(spread) * cross).astype(BF16))
                x_pair = x_ref[here, j * WIDE + k * 128 : j * WIDE + (k + 1) * 128]
                none = jnp.zeros_like(x_pair)
                x_both = jnp.concatenate(
                    [jnp.where(left, x_pair, none), jnp.where(left, none, x_pair)], axis=0
                )
                parts.append(dot(jnp.concatenate(mixes, axis=1), x_both))
            y = jnp.concatenate(parts, axis=1) + read + skip_ref[:, wide] * x_wide
            y_ref[here, wide] = y.astype(BF16)
            weighted = (x_wide * spread_out[SPAN : 2 * SPAN]).astype(BF16)
            carry_ref[:, wide] = spread_out[2 * SPAN : 2 * SPAN + 1] * carry + dot(b_turned, weighted)


def scan_kernel(in_ref, out_ref):
    carry = jnp.zeros((HALF, 128), F32)
    for k in range(PAIRS):
        out_ref[k] = carry.astype(BF16)
        decay = in_ref[k, HALF : HALF + 8, :].astype(F32)
        decay = decay[0:1] + decay[1:2]
        carry = decay * carry + in_ref[k, :HALF, :].astype(F32)


def score_kernel(
    base_ref, valid_ref, keep_ref, got_ref, c_ref, g_ref, y_any, z_any, gain_ref, head_ref,
    q0_ref, q1_ref, q2_ref, q3_ref, pair_ref, score_ref, paired_ref,
    e_ref, mean_ref, best_ref, enter_ref, q_ref, y_ref, z_ref, sems
):
    step = pl.program_id(0)

    def fetches(i):
        rows = pl.ds(i * BLOCK, BLOCK)
        return (
            pltpu.make_async_copy(y_any.at[rows, :], y_ref.at[i], sems.at[0, i]),
            pltpu.make_async_copy(z_any.at[rows, :], z_ref.at[i], sems.at[1, i]),
        )

    @pl.when(step == 0)
    def _():
        for i in range(TOKENS // BLOCK):
            for fetch in fetches(i):
                fetch.start()
        e_ref[...] = head_selector(2 * HEADS, 0, INNER)
        same = (iota((256, 256), 0) >> 6) == (iota((256, 256), 1) >> 6)
        mean_ref[...] = jnp.where(same, 1.0 / HEAD_DIM, 0.0).astype(BF16)
        for d in range(8):
            place = pl.multiple_of((base_ref[2] ^ d) * 16, 16)
            part = (q0_ref, q1_ref, q2_ref, q3_ref)[d // 2]
            for i in range(QTOK):
                q_ref[pl.ds(pl.multiple_of(i * QTOT + place, 16), 16), :] = part[d % 2, i]
        lower = base_ref[1] == 0
        for k in range(PAIRS):
            lanes = slice(k * 128, (k + 1) * 128)
            keep, got = keep_ref[k].astype(F32), got_ref[k].astype(F32)
            enter_ref[:HALF, lanes] = jnp.where(lower, keep, got).astype(BF16)
            enter_ref[HALF:, lanes] = jnp.where(lower, got, keep).astype(BF16)

    for fetch in fetches(step):
        fetch.wait()
    factors, c_part = g_ref[...], c_ref[...]
    embedded = jnp.zeros((BLOCK, EMB), F32)
    for j in range(2):
        wide = slice(j * INNER // 2, (j + 1) * INNER // 2)
        y = y_ref[step, :, wide].astype(F32) + dot(factors, e_ref[:, wide]) * dot(c_part, enter_ref[:, wide])
        z_half = 0.5 * z_ref[step, :, wide].astype(F32)
        gated = y * (z_half + z_half * jnp.tanh(z_half))
        squares = (gated * gated).astype(BF16)
        means = jnp.concatenate(
            [dot(squares[:, k : k + 256], mean_ref[...]) for k in range(0, INNER // 2, 256)], axis=1
        )
        normed = (gated * lax.rsqrt(means + 1e-05) * gain_ref[:, wide]).astype(BF16)
        embedded = embedded + dot(normed, head_ref[wide, :])
    embedded = embedded * lax.rsqrt(jnp.sum(embedded * embedded, axis=1, keepdims=True) + 1e-06)
    for p in range(BLOCK // SPAN):
        passage = step * (BLOCK // SPAN) + p
        vectors = embedded[p * SPAN : (p + 1) * SPAN]
        kept = iota((SPAN, EMB), 0) < valid_ref[0, passage]
        vectors = jnp.where(kept, vectors, vectors[:1]).astype(BF16)
        for j in range(QTOK * QTOT // 1024):
            lanes = slice(j * 1024, (j + 1) * 1024)
            sims = dot_nt(vectors, q_ref[lanes, :])
            best_ref[pl.ds(passage, 1), lanes] = jnp.max(sims, axis=0, keepdims=True)

    @pl.when(step == TOKENS // BLOCK - 1)
    def _():
        total = best_ref[:, :QTOT]
        for i in range(1, QTOK):
            total = total + best_ref[:, i * QTOT : (i + 1) * QTOT]
        score_ref[...] = total
        matched = pair_ref[...] == base_ref[0] + iota((SPANS, QTOT), 0)
        paired = jnp.sum(jnp.where(matched, total, 0.0), axis=0, keepdims=True)
        paired_ref[...] = jnp.broadcast_to(paired, paired_ref.shape)


def whole(shape, space=None):
    kind = {} if space is None else {"memory_space": space}
    return pl.BlockSpec(shape, lambda i: (0,) * len(shape), **kind)


def params(mib):
    return pltpu.CompilerParams(
        dimension_semantics=("arbitrary",), vmem_limit_bytes=mib * 1024 * 1024
    )


def cost(flops, bytes_accessed, transcendentals=0):
    return pl.CostEstimate(
        flops=flops, bytes_accessed=bytes_accessed, transcendentals=transcendentals
    )


def device_states(core, decays, b, x):
    packed = jax.ShapeDtypeStruct((PAIRS, ROWS, 128), BF16)
    far = pl.BlockSpec(memory_space=pltpu.HBM)
    near = pl.BlockSpec(memory_space=pltpu.VMEM)
    return pl.pallas_call(
        states_kernel,
        in_specs=[pl.BlockSpec(memory_space=pltpu.SMEM), far, far, far],
        out_specs=[near, near],
        out_shape=[packed, packed],
        scratch_shapes=[
            pltpu.VMEM((HEADS, TOKENS), F32),
            pltpu.VMEM((TOKENS, STATE), BF16),
            pltpu.VMEM((CHUNKS, TOKENS, WIDE), BF16),
            pltpu.VMEM((TOKENS, 2 * HEADS), BF16),
            pltpu.VMEM((STATE, TOKENS), BF16),
            pltpu.SemaphoreType.DMA((CHUNKS + 2,)),
        ],
        compiler_params=pltpu.CompilerParams(vmem_limit_bytes=60 * 1024 * 1024),
        cost_estimate=cost(10**9, 5 * 10**6),
        name="device_states",
    )(core, decays, b, x)


def local_part(decays, b, c, x, skip):
    def tokens(columns):
        return pl.BlockSpec((TOGETHER * SPAN, columns), lambda i: (i, 0))

    return pl.pallas_call(
        local_kernel,
        grid=(SPANS // TOGETHER,),
        in_specs=[
            whole((HEADS, TOKENS)),
            tokens(STATE),
            tokens(STATE),
            tokens(INNER),
            whole((1, INNER)),
        ],
        out_specs=[tokens(INNER), whole((TOKENS, 2 * HEADS))],
        out_shape=[
            jax.ShapeDtypeStruct((TOKENS, INNER), BF16),
            jax.ShapeDtypeStruct((TOKENS, 2 * HEADS), BF16),
        ],
        scratch_shapes=[
            pltpu.VMEM((STATE, INNER), F32),
            pltpu.VMEM((2 * HEADS, INNER), BF16),
            pltpu.VMEM((SPANS, SPAN, HEADS), F32),
            pltpu.VMEM((SPANS, HEADS, SPAN), F32),
            pltpu.VMEM((SPANS, 2 * SPAN + 16, 2 * HEADS), BF16),
        ],
        compiler_params=params(60),
        cost_estimate=cost(8 * 10**9, 9 * 10**6, 4 * 10**6),
        name="local_part",
    )(decays, b, c, x, skip)


def scan_chips(states):
    return pl.pallas_call(
        scan_kernel,
        out_shape=jax.ShapeDtypeStruct((PAIRS, HALF, 128), BF16),
        compiler_params=pltpu.CompilerParams(vmem_limit_bytes=4 * 1024 * 1024),
        cost_estimate=cost(10**6, 600_000),
        name="scan_chips",
    )(states)


def scores(base, valid_len, keep, got, c, growth, y, z, gain, w_head, q, pair_ids):
    def tokens(width):
        return pl.BlockSpec((BLOCK, width), lambda i: (i, 0))

    smem = pl.BlockSpec(memory_space=pltpu.SMEM)
    far = pl.BlockSpec(memory_space=pltpu.HBM)
    half = whole((PAIRS, HALF, 128))
    everyone = 256
    return pl.pallas_call(
        score_kernel,
        grid=(TOKENS // BLOCK,),
        in_specs=[
            smem,
            smem,
            half,
            half,
            tokens(STATE),
            tokens(2 * HEADS),
            far,
            far,
            whole((1, INNER)),
            whole((INNER, EMB)),
            *[whole((2, QTOK, QTOT // 8, EMB))] * 4,
            whole((1, QTOT)),
        ],
        out_specs=[whole((SPANS, QTOT)), whole((everyone, QTOT))],
        out_shape=[
            jax.ShapeDtypeStruct((SPANS, QTOT), F32),
            jax.ShapeDtypeStruct((everyone, QTOT), F32),
        ],
        scratch_shapes=[
            pltpu.VMEM((2 * HEADS, INNER), BF16),
            pltpu.VMEM((256, 256), BF16),
            pltpu.VMEM((SPANS, QTOK * QTOT), F32),
            pltpu.VMEM((STATE, INNER), BF16),
            pltpu.VMEM((QTOK * QTOT, EMB), BF16),
            pltpu.VMEM((TOKENS // BLOCK, BLOCK, INNER), BF16),
            pltpu.VMEM((TOKENS // BLOCK, BLOCK, INNER), BF16),
            pltpu.SemaphoreType.DMA((2, TOKENS // BLOCK)),
        ],
        compiler_params=params(60),
        cost_estimate=cost(6 * 10**9, 11 * 10**6, 2 * 10**6),
        name="scores",
    )(base, valid_len, keep, got, c, growth, y, z, gain, w_head, *q, pair_ids)


def swap_cores(v):
    return lax.ppermute(v, "core", [(0, 1), (1, 0)])


def decay_of(packed):
    return packed[:, HALF : HALF + 1].astype(F32) + packed[:, HALF + 1 : HALF + 2].astype(F32)


def on_device(
    x_inner, z_gate, b_proj, c_proj, decays, d_skip, norm_gain, w_head, queries, valid_len, pair_ids
):
    core = lax.axis_index("core")
    x, z, b, c, decay = x_inner[0], z_gate[0], b_proj[0], c_proj[0], decays[0]

    own, send = device_states(core.reshape(1), decay, b, x)
    got = swap_cores(send)
    lower = core == 0
    first = jnp.where(lower, own, got)
    second = jnp.where(lower, got, own)
    d_first, d_second = decay_of(first), decay_of(second)
    chip = d_second * first[:, :HALF].astype(F32) + second[:, :HALF].astype(F32)
    high, low = split2(d_first * d_second)
    fill = jnp.zeros((PAIRS, 14, 128), BF16)
    packed = jnp.concatenate([chip.astype(BF16), high, low, fill], axis=1)
    packed, decay, queries = lax.optimization_barrier((packed, decay, queries))
    by_pair = lax.all_to_all(packed, ("z", "y_lo"), 0, 0, tiled=True)

    wide = queries.astype(F32)
    q = (wide * lax.rsqrt(jnp.sum(wide * wide, axis=-1, keepdims=True) + 1e-06)).astype(BF16)
    q = lax.optimization_barrier(q.transpose(1, 0, 2))
    q_pair = jnp.stack([q, lax.ppermute(q, "y_hi", [(0, 1), (1, 0)])])
    document = lax.axis_index(("x", "y_hi"))
    place = lax.axis_index(("z", "y_lo", "core"))
    base = jnp.stack([(document * 32 + place) * SPANS, core, document])
    skip = jnp.repeat(d_skip, HEAD_DIM).reshape(1, INNER)
    y, growth = local_part(decay, b, c, x, skip)
    by_pair, y, growth, q_pair, base = lax.optimization_barrier(
        (by_pair, y, growth, q_pair, base)
    )
    prefix, q_pair = lax.optimization_barrier((scan_chips(by_pair), q_pair))
    entering = lax.all_to_all(prefix, ("z", "y_lo"), 0, 0, tiled=True)
    q_parts = [q_pair] + [
        lax.ppermute(q_pair, "x", [(i, i ^ d) for i in range(4)]) for d in range(1, 4)
    ]
    after = (
        d_first * entering.astype(F32) + first[:, :HALF].astype(F32)
    ).astype(BF16)
    keep = jnp.where(lower, entering, after)
    got = swap_cores(jnp.where(lower, after, entering))

    maxsim, paired = scores(
        base, valid_len, keep, got, c, growth, y, z, norm_gain.reshape(1, INNER), w_head, q_parts,
        pair_ids.reshape(1, QTOT),
    )
    everything = lax.all_to_all(paired, ("z", "y_lo", "core", "x", "y_hi"), 0, 0, tiled=True)
    return maxsim[None], jnp.sum(everything, axis=0)


def solution(mesh):
    cut = Mesh(mesh.devices.reshape(8, 2, 2, 4, 2), ("z", "y_lo", "core", "x", "y_hi"))
    seq, qry = ("z", "y_lo", "core"), ("x", "y_hi")
    return jax.shard_map(
        on_device,
        mesh=cut,
        in_specs=(
            P(qry, seq, None),
            P(qry, seq, None),
            P(qry, seq, None),
            P(qry, seq, None),
            P(qry, None, seq),
            P(),
            P(),
            P(),
            P(qry, None, None),
            P(qry, seq),
            P(),
        ),
        out_specs=(P(qry, seq, None), P()),
        check_vma=False,
    )
```

time: 122 us -> 99.7 us (0.82)
  local copies, waits for them, and re-layouts: 18.7 us -> 1.53 us
  blocking collectives: 41.4 us -> 25.4 us
  starting transfers between devices: 17 us -> 27.2 us
  waiting for transfers between devices: 11.3 us -> 7.71 us
  Pallas kernels: 30 us -> 32.1 us
  other arithmetic: 2.44 us -> 4.52 us
    all_to_all x1 -> x0, blocking collectives: 19.8 us -> none  [on_device(): by_pair = lax.all_to_all(packed, ('z', 'y_lo'), 0, 0, tiled=True)]
    unnamed x36 -> x14, local copies, waits for them, and re-layouts: 16.8 us -> 0.71 us
    ppermute x0 -> x4, starting transfers between devices: none -> 6.05 us  [the longest x3 3.34 us: on_device(): lax.ppermute(q_pair, 'x', [(i, i ^ d) for i in range(4)])]
    all_to_all x2, starting transfers between devices: 10.2 us -> 14.5 us  [the longest x1 7.57 us: on_device(): by_pair = lax.all_to_all(packed, ('z', 'y_lo'), 0, 0, tiled=True)]
    all_to_all x1, blocking collectives: 21.6 us -> 25.4 us  [on_device(): lax.all_to_all(paired, ('z', 'y_lo', 'core', 'x', 'y_hi'), 0, 0, tiled=True)]
    all_to_all x2, waiting for transfers between devices: 9.39 us -> 6.5 us  [the longest x1 6.5 us: on_device(): entering = lax.all_to_all(prefix, ('z', 'y_lo'), 0, 0, tiled=True)]
    pallas_call x1, Pallas kernels: 11.5 us -> 14.2 us  [scores(): pl.pallas_call(score_kernel, grid=(TOKENS // BLOCK,), in_specs=[smem, sme...]
  transfers between devices with their start and end apart: 4 -> 8, of which waited for: 3 -> 3; matrix products, arithmetic and copies ran while one was open for 2% -> 3% of each run, Pallas kernels for 11% -> 12%
where the time goes in v1:
time: 99.7 us; the launch traced here: 99.3 us
  Pallas kernels  32.1 us (32%)
  starting transfers between devices  27.2 us (27%)
  blocking collectives  25.4 us (25%)
  waiting for transfers between devices  7.71 us (8%)
  other arithmetic  4.52 us (5%)
  local copies, waits for them, and re-layouts  1.53 us (2%)
    all_to_all x1, blocking collectives, on_device(): lax.all_to_all(paired, ('z', 'y_lo', 'core', 'x', 'y_hi'), 0, 0, tiled=True)  25.4 us
    pallas_call x1, Pallas kernels, scores(): pl.pallas_call(score_kernel, grid=(TOKENS // BLOCK,), in_specs=[smem, sme...  14.2 us
    pallas_call x1, Pallas kernels, local_part(): pl.pallas_call(local_kernel, grid=(SPANS // TOGETHER,), in_specs=[whole((...  11.9 us
    all_to_all x1, starting transfers between devices, on_device(): by_pair = lax.all_to_all(packed, ('z', 'y_lo'), 0, 0, tiled=True)  7.57 us
    all_to_all x1, starting transfers between devices, on_device(): entering = lax.all_to_all(prefix, ('z', 'y_lo'), 0, 0, tiled=True)  6.95 us
    ppermute x2, starting transfers between devices, swap_cores(): return lax.ppermute(v, 'core', [(0, 1), (1, 0)])  6.59 us
    all_to_all x1, waiting for transfers between devices, on_device(): entering = lax.all_to_all(prefix, ('z', 'y_lo'), 0, 0, tiled=True)  6.5 us
    pallas_call x1, Pallas kernels, device_states(): pl.pallas_call(states_kernel, in_specs=[pl.BlockSpec(memory_space=pltpu.S...  5.18 us
  transfers between devices with their start and end apart: 8, of which 3 were waited for; matrix products, arithmetic and copies ran while one was open for 3% of the time, Pallas kernels for 12%

profile of v1, /device:TPU:1, one launch (start us, length us, event | category | flops | bytes accessed | tf_op | source)
XLA Modules:
  0.0 99.3 jit_solution(1333142880851958826)
XLA Ops:
  0.7 5.2 %device_states.1 = (bf16[16,80,128]{2,1,0:T(8,128)(2,1)}, bf16[16,80,128]{2,1,0:T(8,128)(2,1)}) custom-call(s32[1]{0:T(128)} %bitcast.core_ref, f32[32,1024]{1,0:T(8,128)} %bitcast.25, bf16[1024,128]{1,0:T(8,128)(2,1)} %bitcast.23, bf16[1024,2048]{1,0:T(8,128)(2,1)} %bitcast.20), custom_call_target="tpu_custom_call" | custom-call | flops 1000000000 | bytes 5000000 | tf_op jit(solution)/shard_map/device_states/pallas_call | solution.py:286
  5.8 3.3 %collective-permute-start = (bf16[16,80,128]{2,1,0:T(8,128)(2,1)}, bf16[16,80,128]{2,1,0:T(8,128)(2,1)S(1)}, u32[]{:S(2)}, u32[]{:S(2)}) collective-permute-start(bf16[16,80,128]{2,1,0:T(8,128)(2,1)} %get-tuple-element.18), channel_id=1, source_target_pairs={{0,8},{8,0},{1,9},{9,1},{2,10},{10,2},{3,11},{11,3},{4,12},{12,4},... | collective-permute-start | bytes 983048 | tf_op jit(solution)/shard_map/ppermute | solution.py:394
  9.2 0.1 broadcast_in_dim.11
  9.2 0.7 reshape_reshape.3.skip_ref
  9.9 0.1 pad.8.clone
  10.0 0.6 pad_add_fusion.base_ref
  10.6 0.1 collective-permute-done
  10.6 1.0 %broadcast_select_fusion = (bf16[16,80,128]{2,1,0:T(8,128)(2,1)S(1)}, bf16[16,80,128]{2,1,0:T(8,128)(2,1)S(1)}) fusion(bf16[16,80,128]{2,1,0:T(8,128)(2,1)} %get-tuple-element.19, bf16[16,80,128]{2,1,0:T(8,128)(2,1)S(1)} %collective-permute-done, pred[]{:T(512)S(6)} %eq.3), kind=kLoop, calls=%fused_computation.10 | loop fusion | flops 327680 | bytes 1310721 | tf_op jit(solution)/shard_map/jit(_where)/select_n | solution.py:410
  11.7 0.1 fusion.1
  11.8 0.9 maximum_maximum_fusion
  12.7 7.6 %all-to-all-start = ((bf16[16,80,128]{2,1,0:T(8,128)(2,1)}), bf16[16,80,128]{2,1,0:T(8,128)(2,1)S(1)}, u32[]{:S(2)}, u32[]{:S(2)}) async-start(bf16[16,80,128]{2,1,0:T(8,128)(2,1)} %maximum_maximum_fusion), calls=%async_computation | async-start | bytes 655360 | tf_op jit(solution)/shard_map/all_to_all | solution.py:418
  20.3 0.1 fusion.5
  20.4 0.1 fusion.7
  20.6 2.7 %collective-permute-start.1 = (bf16[32,16,128]{2,1,0:T(8,128)(2,1)S(1)}, bf16[32,16,128]{2,1,0:T(8,128)(2,1)S(1)}, u32[]{:S(2)}, u32[]{:S(2)}) collective-permute-start(bf16[32,16,128]{2,1,0:T(8,128)(2,1)S(1)} %fusion.7), channel_id=1, source_target_pairs={{0,1},{1,0},{2,3},{3,2},{4,5},{5,4},{6,7},{7,6},{8,9},{9,8},{10,11... | collective-permute-start | bytes 393224 | tf_op jit(solution)/shard_map/ppermute | solution.py:423
  23.3 11.9 %local_part.1 = (bf16[1024,2048]{1,0:T(8,128)(2,1)}, bf16[1024,64]{1,0:T(8,128)(2,1)}) custom-call(f32[32,1024]{1,0:T(8,128)} %bitcast.26, bf16[1024,128]{1,0:T(8,128)(2,1)} %bitcast.24, bf16[1024,128]{1,0:T(8,128)(2,1)} %bitcast.32, bf16[1024,2048]{1,0:T(8,128)(2,1)} %bitcast.21, f32[1,2048]{1,0:T(1,128)} %reshape_reshape.3.skip_ref), custom_call_target="tpu_custom_call" | custom-call | flops 8000000000 | bytes 9000000 | tf_op jit(solution)/shard_map/local_part/pallas_call | solution.py:309
  35.1 0.0 collective-permute-done.1
  35.2 0.0 all-to-all-done.in_ref
  35.2 0.8 scan_chips.1
  36.0 7.0 %all-to-all-start.1 = ((bf16[16,64,128]{2,1,0:T(8,128)(2,1)}), bf16[16,64,128]{2,1,0:T(8,128)(2,1)S(1)}, u32[]{:S(2)}, u32[]{:S(2)}) async-start(bf16[16,64,128]{2,1,0:T(8,128)(2,1)} %scan_chips.1), calls=%async_computation.1 | async-start | bytes 524288 | tf_op jit(solution)/shard_map/all_to_all | solution.py:433
  43.0 2.6 %collective-permute-start.5 = (bf16[2,32,16,128]{3,2,1,0:T(8,128)(2,1)S(1)}, bf16[2,32,16,128]{3,2,1,0:T(8,128)(2,1)S(1)}, u32[]{:S(2)}, u32[]{:S(2)}) collective-permute-start(bf16[2,32,16,128]{3,2,1,0:T(8,128)(2,1)S(1)} %pad_maximum_fusion.q0_ref), channel_id=1, source_target_pairs={{0,6},{2,4},{4,2},{6,0},{1,7},{3,5},{5,3},{7,1},{8,14},{10,12},{12... | collective-permute-start | bytes 786440 | tf_op jit(solution)/shard_map/ppermute | solution.py:435
  45.5 0.5 collective-permute-start.4
  46.0 0.3 collective-permute-start.3
  46.3 6.5 %all-to-all-done.1 = bf16[16,64,128]{2,1,0:T(8,128)(2,1)S(1)} async-done(((bf16[16,64,128]{2,1,0:T(8,128)(2,1)}), bf16[16,64,128]{2,1,0:T(8,128)(2,1)S(1)}, u32[]{:S(2)}, u32[]{:S(2)}) %all-to-all-start.1) | async-done | bytes 262176 | tf_op jit(solution)/shard_map/all_to_all | solution.py:433
  52.8 0.8 fusion.3
  53.6 3.3 %collective-permute-start.2 = (bf16[16,64,128]{2,1,0:T(8,128)(2,1)S(1)}, bf16[16,64,128]{2,1,0:T(8,128)(2,1)S(1)}, u32[]{:S(2)}, u32[]{:S(2)}) collective-permute-start(bf16[16,64,128]{2,1,0:T(8,128)(2,1)S(1)} %get-tuple-element.39), channel_id=1, source_target_pairs={{0,8},{8,0},{1,9},{9,1},{2,10},{10,2},{3,11},{11,3},{4,12},{12,4},... | collective-permute-start | bytes 786440 | tf_op jit(solution)/shard_map/ppermute | solution.py:394
  56.9 0.0 collective-permute-done.5.q3_ref
  56.9 0.0 collective-permute-done.4.q2_ref
  57.0 1.1 %collective-permute-done.2.got_ref = bf16[16,64,128]{2,1,0:T(8,128)(2,1)S(1)} collective-permute-done((bf16[16,64,128]{2,1,0:T(8,128)(2,1)S(1)}, bf16[16,64,128]{2,1,0:T(8,128)(2,1)S(1)}, u32[]{:S(2)}, u32[]{:S(2)}) %collective-permute-start.2) | collective-permute-done | bytes 262176 | tf_op jit(solution)/shard_map/ppermute | solution.py:394
  58.1 0.7 copy-done.6
  58.8 14.2 %scores.1 = (f32[8,128]{1,0:T(8,128)}, f32[256,128]{1,0:T(8,128)}) custom-call(s32[3]{0:T(128)} %pad_add_fusion.base_ref, s32[1,8]{1,0:T(1,128)} %valid_ref.1, bf16[16,64,128]{2,1,0:T(8,128)(2,1)} %get-tuple-element.40.keep_ref, bf16[16,64,128]{2,1,0:T(8,128)(2,1)} %copy-done.6, bf16[1024,128]{1,0:T(8,128)(2,1)} %bitcast.33, ...), custom_call_target="tpu_custom_call" | custom-call | flops 6000000000 | bytes 11000000 | tf_op jit(solution)/shard_map/scores/pallas_call | solution.py:355
  73.0 25.4 %all_to_all.19 = f32[256,1,128]{2,1,0:T(1,128)S(1)} all-to-all(f32[256,1,128]{2,1,0:T(1,128)} %bitcast.27), channel_id=1, replica_groups=mesh['z'=8,'y_lo'=2,'core'=2,'x'=4,'y_hi'=2] {'z','y_lo','core','x','y_hi'}, dimensions={0} | all-to-all | bytes 262144 | tf_op jit(solution)/shard_map/all_to_all | solution.py:447
  98.5 0.8 reduce_sum.19
  (19 shorter events, 0.1 us)
Async XLA Ops:
  0.6 8.5 %copy-start.2 = (f32[32]{0:T(128)S(1)}, f32[32]{0:T(128)}, u32[]{:S(2)}) copy-start(f32[32]{0:T(128)} %param.16) | copy-start | bytes 388
  0.6 19.6 %copy-start = (bf16[16,32,128]{2,1,0:T(8,128)(2,1)S(1)}, bf16[16,32,128]{2,1,0:T(8,128)(2,1)}, u32[]{:S(2)}) copy-start(bf16[16,32,128]{2,1,0:T(8,128)(2,1)} %param.19) | copy-start | bytes 393220
  5.8 4.8 %collective-permute-start = (bf16[16,80,128]{2,1,0:T(8,128)(2,1)}, bf16[16,80,128]{2,1,0:T(8,128)(2,1)S(1)}, u32[]{:S(2)}, u32[]{:S(2)}) collective-permute-start(bf16[16,80,128]{2,1,0:T(8,128)(2,1)} %get-tuple-element.18), channel_id=1, source_target_pairs={{0,8},{8,0},{1,9},{9,1},{2,10},{10,2},{3,11},{11,3},{4,12},{12,4},... | collective-permute-start | bytes 983048 | tf_op jit(solution)/shard_map/ppermute | solution.py:394
  12.7 22.5 %all-to-all-start = ((bf16[16,80,128]{2,1,0:T(8,128)(2,1)}), bf16[16,80,128]{2,1,0:T(8,128)(2,1)S(1)}, u32[]{:S(2)}, u32[]{:S(2)}) async-start(bf16[16,80,128]{2,1,0:T(8,128)(2,1)} %maximum_maximum_fusion), calls=%async_computation | async-start | bytes 655360 | tf_op jit(solution)/shard_map/all_to_all | solution.py:418
  20.6 14.6 %collective-permute-start.1 = (bf16[32,16,128]{2,1,0:T(8,128)(2,1)S(1)}, bf16[32,16,128]{2,1,0:T(8,128)(2,1)S(1)}, u32[]{:S(2)}, u32[]{:S(2)}) collective-permute-start(bf16[32,16,128]{2,1,0:T(8,128)(2,1)S(1)} %fusion.7), channel_id=1, source_target_pairs={{0,1},{1,0},{2,3},{3,2},{4,5},{5,4},{6,7},{7,6},{8,9},{9,8},{10,11... | collective-permute-start | bytes 393224 | tf_op jit(solution)/shard_map/ppermute | solution.py:423
  35.2 22.9 %copy-start.1 = (bf16[2,32,16,128]{3,2,1,0:T(8,128)(2,1)}, bf16[2,32,16,128]{3,2,1,0:T(8,128)(2,1)S(1)}, u32[]{:S(2)}) copy-start(bf16[2,32,16,128]{3,2,1,0:T(8,128)(2,1)S(1)} %pad_maximum_fusion.q0_ref) | copy-start | bytes 786436
  36.0 16.8 %all-to-all-start.1 = ((bf16[16,64,128]{2,1,0:T(8,128)(2,1)}), bf16[16,64,128]{2,1,0:T(8,128)(2,1)S(1)}, u32[]{:S(2)}, u32[]{:S(2)}) async-start(bf16[16,64,128]{2,1,0:T(8,128)(2,1)} %scan_chips.1), calls=%async_computation.1 | async-start | bytes 524288 | tf_op jit(solution)/shard_map/all_to_all | solution.py:433
  43.0 14.0 %collective-permute-start.5 = (bf16[2,32,16,128]{3,2,1,0:T(8,128)(2,1)S(1)}, bf16[2,32,16,128]{3,2,1,0:T(8,128)(2,1)S(1)}, u32[]{:S(2)}, u32[]{:S(2)}) collective-permute-start(bf16[2,32,16,128]{3,2,1,0:T(8,128)(2,1)S(1)} %pad_maximum_fusion.q0_ref), channel_id=1, source_target_pairs={{0,6},{2,4},{4,2},{6,0},{1,7},{3,5},{5,3},{7,1},{8,14},{10,12},{12... | collective-permute-start | bytes 786440 | tf_op jit(solution)/shard_map/ppermute | solution.py:435
  45.5 11.4 %collective-permute-start.4 = (bf16[2,32,16,128]{3,2,1,0:T(8,128)(2,1)S(1)}, bf16[2,32,16,128]{3,2,1,0:T(8,128)(2,1)S(1)}, u32[]{:S(2)}, u32[]{:S(2)}) collective-permute-start(bf16[2,32,16,128]{3,2,1,0:T(8,128)(2,1)S(1)} %pad_maximum_fusion.q0_ref), channel_id=1, source_target_pairs={{0,4},{2,6},{4,0},{6,2},{1,5},{3,7},{5,1},{7,3},{8,12},{10,14},{12... | collective-permute-start | bytes 786440 | tf_op jit(solution)/shard_map/ppermute | solution.py:435
  46.0 10.9 %collective-permute-start.3 = (bf16[2,32,16,128]{3,2,1,0:T(8,128)(2,1)S(1)}, bf16[2,32,16,128]{3,2,1,0:T(8,128)(2,1)S(1)}, u32[]{:S(2)}, u32[]{:S(2)}) collective-permute-start(bf16[2,32,16,128]{3,2,1,0:T(8,128)(2,1)S(1)} %pad_maximum_fusion.q0_ref), channel_id=1, source_target_pairs={{0,2},{2,0},{4,6},{6,4},{1,3},{3,1},{5,7},{7,5},{8,10},{10,8},{12,... | collective-permute-start | bytes 786440 | tf_op jit(solution)/shard_map/ppermute | solution.py:435
  53.6 4.4 %collective-permute-start.2 = (bf16[16,64,128]{2,1,0:T(8,128)(2,1)S(1)}, bf16[16,64,128]{2,1,0:T(8,128)(2,1)S(1)}, u32[]{:S(2)}, u32[]{:S(2)}) collective-permute-start(bf16[16,64,128]{2,1,0:T(8,128)(2,1)S(1)} %get-tuple-element.39), channel_id=1, source_target_pairs={{0,8},{8,0},{1,9},{9,1},{2,10},{10,2},{3,11},{11,3},{4,12},{12,4},... | collective-permute-start | bytes 786440 | tf_op jit(solution)/shard_map/ppermute | solution.py:394
  56.9 1.2 %copy-start.3 = (bf16[2,32,16,128]{3,2,1,0:T(8,128)(2,1)}, bf16[2,32,16,128]{3,2,1,0:T(8,128)(2,1)S(1)}, u32[]{:S(2)}) copy-start(bf16[2,32,16,128]{3,2,1,0:T(8,128)(2,1)S(1)} %collective-permute-done.5.q3_ref) | copy-start | bytes 786436
  56.9 1.2 %copy-start.4 = (bf16[2,32,16,128]{3,2,1,0:T(8,128)(2,1)}, bf16[2,32,16,128]{3,2,1,0:T(8,128)(2,1)S(1)}, u32[]{:S(2)}) copy-start(bf16[2,32,16,128]{3,2,1,0:T(8,128)(2,1)S(1)} %collective-permute-done.4.q2_ref) | copy-start | bytes 786436
  56.9 1.1 %copy-start.5 = (bf16[2,32,16,128]{3,2,1,0:T(8,128)(2,1)}, bf16[2,32,16,128]{3,2,1,0:T(8,128)(2,1)S(1)}, u32[]{:S(2)}) copy-start(bf16[2,32,16,128]{3,2,1,0:T(8,128)(2,1)S(1)} %collective-permute-done.3.q1_ref) | copy-start | bytes 786436
  58.1 0.7 copy-start.6

commit v2 on v1

--- a/solution.py
+++ b/solution.py
@@ -384,7 +384,7 @@
             pltpu.VMEM((TOKENS // BLOCK, BLOCK, INNER), BF16),
             pltpu.SemaphoreType.DMA((2, TOKENS // BLOCK)),
         ],
-        compiler_params=params(60),
+        compiler_params=params(50),
         cost_estimate=cost(6 * 10**9, 11 * 10**6, 2 * 10**6),
         name="scores",
     )(base, valid_len, keep, got, c, growth, y, z, gain, w_head, *q, pair_ids)
@@ -414,7 +414,9 @@
     high, low = split2(d_first * d_second)
     fill = jnp.zeros((PAIRS, 14, 128), BF16)
     packed = jnp.concatenate([chip.astype(BF16), high, low, fill], axis=1)
-    packed, decay, queries = lax.optimization_barrier((packed, decay, queries))
+    packed, decay, queries, d_skip, own_core = lax.optimization_barrier(
+        (packed, decay, queries, d_skip, core)
+    )
     by_pair = lax.all_to_all(packed, ("z", "y_lo"), 0, 0, tiled=True)
 
     wide = queries.astype(F32)
@@ -423,7 +425,7 @@
     q_pair = jnp.stack([q, lax.ppermute(q, "y_hi", [(0, 1), (1, 0)])])
     document = lax.axis_index(("x", "y_hi"))
     place = lax.axis_index(("z", "y_lo", "core"))
-    base = jnp.stack([(document * 32 + place) * SPANS, core, document])
+    base = jnp.stack([(document * 32 + place) * SPANS, own_core, document])
     skip = jnp.repeat(d_skip, HEAD_DIM).reshape(1, INNER)
     y, growth = local_part(decay, b, c, x, skip)
     by_pair, y, growth, q_pair, base = lax.optimization_barrier(

time: 99.7 us -> 99.4 us (level)
  waiting for transfers between devices: 7.71 us -> 9.05 us
  other arithmetic: 4.52 us -> 3.34 us
  Pallas kernels: 32.1 us -> 31 us
    ppermute x2, waiting for transfers between devices: 1.2 us -> 2.37 us  [swap_cores(): return lax.ppermute(v, 'core', [(0, 1), (1, 0)])]
    pallas_call x1, Pallas kernels: 14.2 us -> 13.1 us  [scores(): pl.pallas_call(score_kernel, grid=(TOKENS // BLOCK,), in_specs=[smem, sme...]
  transfers between devices with their start and end apart: 8 -> 8, of which waited for: 3 -> 4; matrix products, arithmetic and copies ran while one was open for 3% -> 1% of each run, Pallas kernels for 12% -> 12%
where the time goes in v2:
time: 99.4 us; the launch traced here: 99 us
  Pallas kernels  31 us (31%)
  starting transfers between devices  27.4 us (28%)
  blocking collectives  25.6 us (26%)
  waiting for transfers between devices  9.05 us (9%)
  other arithmetic  3.34 us (3%)
  local copies, waits for them, and re-layouts  1.8 us (2%)
    all_to_all x1, blocking collectives, on_device(): lax.all_to_all(paired, ('z', 'y_lo', 'core', 'x', 'y_hi'), 0, 0, tiled=True)  25.6 us
    pallas_call x1, Pallas kernels, scores(): pl.pallas_call(score_kernel, grid=(TOKENS // BLOCK,), in_specs=[smem, sme...  13.1 us
    pallas_call x1, Pallas kernels, local_part(): pl.pallas_call(local_kernel, grid=(SPANS // TOGETHER,), in_specs=[whole((...  11.9 us
    all_to_all x1, starting transfers between devices, on_device(): by_pair = lax.all_to_all(packed, ('z', 'y_lo'), 0, 0, tiled=True)  7.57 us
    all_to_all x1, starting transfers between devices, on_device(): entering = lax.all_to_all(prefix, ('z', 'y_lo'), 0, 0, tiled=True)  6.94 us
    ppermute x2, starting transfers between devices, swap_cores(): return lax.ppermute(v, 'core', [(0, 1), (1, 0)])  6.87 us
    all_to_all x1, waiting for transfers between devices, on_device(): entering = lax.all_to_all(prefix, ('z', 'y_lo'), 0, 0, tiled=True)  6.5 us
    pallas_call x1, Pallas kernels, device_states(): pl.pallas_call(states_kernel, in_specs=[pl.BlockSpec(memory_space=pltpu.S...  5.17 us
  transfers between devices with their start and end apart: 8, of which 4 were waited for; matrix products, arithmetic and copies ran while one was open for 1% of the time, Pallas kernels for 12%

profile of v2, /device:TPU:1, one launch (start us, length us, event | category | flops | bytes accessed | tf_op | source)
XLA Modules:
  0.0 99.0 jit_solution(2034255197858575259)
XLA Ops:
  0.7 5.2 %device_states.1 = (bf16[16,80,128]{2,1,0:T(8,128)(2,1)}, bf16[16,80,128]{2,1,0:T(8,128)(2,1)}) custom-call(s32[1]{0:T(128)} %bitcast.core_ref, f32[32,1024]{1,0:T(8,128)} %bitcast.31, bf16[1024,128]{1,0:T(8,128)(2,1)} %bitcast.29, bf16[1024,2048]{1,0:T(8,128)(2,1)} %bitcast.26), custom_call_target="tpu_custom_call" | custom-call | flops 1000000000 | bytes 5000000 | tf_op jit(solution)/shard_map/device_states/pallas_call | solution.py:286
  5.8 3.3 %collective-permute-start = (bf16[16,80,128]{2,1,0:T(8,128)(2,1)}, bf16[16,80,128]{2,1,0:T(8,128)(2,1)S(1)}, u32[]{:S(2)}, u32[]{:S(2)}) collective-permute-start(bf16[16,80,128]{2,1,0:T(8,128)(2,1)} %get-tuple-element.20), channel_id=1, source_target_pairs={{0,8},{8,0},{1,9},{9,1},{2,10},{10,2},{3,11},{11,3},{4,12},{12,4},... | collective-permute-start | bytes 983048 | tf_op jit(solution)/shard_map/ppermute | solution.py:394
  9.2 0.1 pad.8.clone
  9.2 1.4 %collective-permute-done = bf16[16,80,128]{2,1,0:T(8,128)(2,1)S(1)} collective-permute-done((bf16[16,80,128]{2,1,0:T(8,128)(2,1)}, bf16[16,80,128]{2,1,0:T(8,128)(2,1)S(1)}, u32[]{:S(2)}, u32[]{:S(2)}) %collective-permute-start) | collective-permute-done | bytes 327712 | tf_op jit(solution)/shard_map/ppermute | solution.py:394
  10.6 1.0 %broadcast_select_fusion = (bf16[16,80,128]{2,1,0:T(8,128)(2,1)S(1)}, bf16[16,80,128]{2,1,0:T(8,128)(2,1)S(1)}) fusion(bf16[16,80,128]{2,1,0:T(8,128)(2,1)} %get-tuple-element.21, bf16[16,80,128]{2,1,0:T(8,128)(2,1)S(1)} %collective-permute-done, pred[]{:T(512)S(6)} %eq.3), kind=kLoop, calls=%fused_computation.10 | loop fusion | flops 327680 | bytes 1310721 | tf_op jit(solution)/shard_map/jit(_where)/select_n | solution.py:410
  11.7 0.1 fusion.1
  11.8 0.9 maximum_maximum_fusion
  12.7 7.6 %all-to-all-start = ((bf16[16,80,128]{2,1,0:T(8,128)(2,1)}), bf16[16,80,128]{2,1,0:T(8,128)(2,1)S(1)}, u32[]{:S(2)}, u32[]{:S(2)}) async-start(bf16[16,80,128]{2,1,0:T(8,128)(2,1)} %maximum_maximum_fusion), calls=%async_computation | async-start | bytes 655360 | tf_op jit(solution)/shard_map/all_to_all | solution.py:420
  20.3 0.1 broadcast_in_dim.11
  20.3 0.7 reshape_reshape.3.skip_ref
  21.0 0.1 fusion.5
  21.2 0.1 fusion.7
  21.3 2.7 %collective-permute-start.1 = (bf16[32,16,128]{2,1,0:T(8,128)(2,1)S(1)}, bf16[32,16,128]{2,1,0:T(8,128)(2,1)S(1)}, u32[]{:S(2)}, u32[]{:S(2)}) collective-permute-start(bf16[32,16,128]{2,1,0:T(8,128)(2,1)S(1)} %fusion.7), channel_id=1, source_target_pairs={{0,1},{1,0},{2,3},{3,2},{4,5},{5,4},{6,7},{7,6},{8,9},{9,8},{10,11... | collective-permute-start | bytes 393224 | tf_op jit(solution)/shard_map/ppermute | solution.py:425
  24.0 0.0 copy-start.4
  24.0 11.9 %local_part.1 = (bf16[1024,2048]{1,0:T(8,128)(2,1)}, bf16[1024,64]{1,0:T(8,128)(2,1)}) custom-call(f32[32,1024]{1,0:T(8,128)} %bitcast.32, bf16[1024,128]{1,0:T(8,128)(2,1)} %bitcast.30, bf16[1024,128]{1,0:T(8,128)(2,1)} %bitcast.22, bf16[1024,2048]{1,0:T(8,128)(2,1)} %bitcast.27, f32[1,2048]{1,0:T(1,128)} %reshape_reshape.3.skip_ref), custom_call_target="tpu_custom_call" | custom-call | flops 8000000000 | bytes 9000000 | tf_op jit(solution)/shard_map/local_part/pallas_call | solution.py:309
  36.0 0.1 pad_add_fusion.base_ref
  36.1 0.8 scan_chips.1
  36.9 6.9 %all-to-all-start.1 = ((bf16[16,64,128]{2,1,0:T(8,128)(2,1)}), bf16[16,64,128]{2,1,0:T(8,128)(2,1)S(1)}, u32[]{:S(2)}, u32[]{:S(2)}) async-start(bf16[16,64,128]{2,1,0:T(8,128)(2,1)} %scan_chips.1), calls=%async_computation.1 | async-start | bytes 524288 | tf_op jit(solution)/shard_map/all_to_all | solution.py:435
  43.8 2.6 %collective-permute-start.5 = (bf16[2,32,16,128]{3,2,1,0:T(8,128)(2,1)S(1)}, bf16[2,32,16,128]{3,2,1,0:T(8,128)(2,1)S(1)}, u32[]{:S(2)}, u32[]{:S(2)}) collective-permute-start(bf16[2,32,16,128]{3,2,1,0:T(8,128)(2,1)S(1)} %pad_maximum_fusion.q0_ref), channel_id=1, source_target_pairs={{0,6},{2,4},{4,2},{6,0},{1,7},{3,5},{5,3},{7,1},{8,14},{10,12},{12... | collective-permute-start | bytes 786440 | tf_op jit(solution)/shard_map/ppermute | solution.py:437
  46.4 0.5 collective-permute-start.4
  46.9 0.2 collective-permute-start.3
  47.2 6.5 %all-to-all-done.1 = bf16[16,64,128]{2,1,0:T(8,128)(2,1)S(1)} async-done(((bf16[16,64,128]{2,1,0:T(8,128)(2,1)}), bf16[16,64,128]{2,1,0:T(8,128)(2,1)S(1)}, u32[]{:S(2)}, u32[]{:S(2)}) %all-to-all-start.1) | async-done | bytes 262176 | tf_op jit(solution)/shard_map/all_to_all | solution.py:435
  53.7 0.1 fusion.3
  53.8 3.5 %collective-permute-start.2 = (bf16[16,64,128]{2,1,0:T(8,128)(2,1)S(1)}, bf16[16,64,128]{2,1,0:T(8,128)(2,1)S(1)}, u32[]{:S(2)}, u32[]{:S(2)}) collective-permute-start(bf16[16,64,128]{2,1,0:T(8,128)(2,1)S(1)} %get-tuple-element.43), channel_id=1, source_target_pairs={{0,8},{8,0},{1,9},{9,1},{2,10},{10,2},{3,11},{11,3},{4,12},{12,4},... | collective-permute-start | bytes 786440 | tf_op jit(solution)/shard_map/ppermute | solution.py:394
  57.4 0.2 collective-permute-done.5.q3_ref
  57.5 0.0 collective-permute-done.4.q2_ref
  57.5 0.0 collective-permute-done.3.q1_ref
  57.5 1.0 collective-permute-done.2.got_ref
  58.5 0.9 copy-done.5
  59.5 13.1 %scores.1 = (f32[8,128]{1,0:T(8,128)}, f32[256,128]{1,0:T(8,128)S(1)}) custom-call(s32[3]{0:T(128)S(1)} %pad_add_fusion.base_ref, s32[1,8]{1,0:T(1,128)S(1)} %copy-done.3, bf16[16,64,128]{2,1,0:T(8,128)(2,1)S(1)} %get-tuple-element.44.keep_ref, bf16[16,64,128]{2,1,0:T(8,128)(2,1)S(1)} %collective-permute-done.2.got_ref, bf16[1024,128]{1,0:T(8,128)(2,1)S(1)} %bitcast.23, ...), custom_call_target="tpu_custom_call" | custom-call | flops 6000000000 | bytes 11000000 | tf_op jit(solution)/shard_map/scores/pallas_call | solution.py:355
  72.6 25.6 %all_to_all.19 = f32[256,1,128]{2,1,0:T(1,128)S(1)} all-to-all(f32[256,1,128]{2,1,0:T(1,128)S(1)} %bitcast.21), channel_id=1, replica_groups=mesh['z'=8,'y_lo'=2,'core'=2,'x'=4,'y_hi'=2] {'z','y_lo','core','x','y_hi'}, dimensions={0} | all-to-all | bytes 262144 | tf_op jit(solution)/shard_map/all_to_all | solution.py:449
  98.2 0.8 reduce_sum.19
  (21 shorter events, 0.1 us)
Async XLA Ops:
  0.6 20.4 %copy-start.6 = (bf16[16,32,128]{2,1,0:T(8,128)(2,1)S(1)}, bf16[16,32,128]{2,1,0:T(8,128)(2,1)}, u32[]{:S(2)}) copy-start(bf16[16,32,128]{2,1,0:T(8,128)(2,1)} %param.19) | copy-start | bytes 393220
  0.6 19.6 %copy-start.7 = (f32[32]{0:T(128)S(1)}, f32[32]{0:T(128)}, u32[]{:S(2)}) copy-start(f32[32]{0:T(128)} %param.16) | copy-start | bytes 388
  5.8 4.8 %collective-permute-start = (bf16[16,80,128]{2,1,0:T(8,128)(2,1)}, bf16[16,80,128]{2,1,0:T(8,128)(2,1)S(1)}, u32[]{:S(2)}, u32[]{:S(2)}) collective-permute-start(bf16[16,80,128]{2,1,0:T(8,128)(2,1)} %get-tuple-element.20), channel_id=1, source_target_pairs={{0,8},{8,0},{1,9},{9,1},{2,10},{10,2},{3,11},{11,3},{4,12},{12,4},... | collective-permute-start | bytes 983048 | tf_op jit(solution)/shard_map/ppermute | solution.py:394
  12.7 23.4 %all-to-all-start = ((bf16[16,80,128]{2,1,0:T(8,128)(2,1)}), bf16[16,80,128]{2,1,0:T(8,128)(2,1)S(1)}, u32[]{:S(2)}, u32[]{:S(2)}) async-start(bf16[16,80,128]{2,1,0:T(8,128)(2,1)} %maximum_maximum_fusion), calls=%async_computation | async-start | bytes 655360 | tf_op jit(solution)/shard_map/all_to_all | solution.py:420
  21.3 14.8 %collective-permute-start.1 = (bf16[32,16,128]{2,1,0:T(8,128)(2,1)S(1)}, bf16[32,16,128]{2,1,0:T(8,128)(2,1)S(1)}, u32[]{:S(2)}, u32[]{:S(2)}) collective-permute-start(bf16[32,16,128]{2,1,0:T(8,128)(2,1)S(1)} %fusion.7), channel_id=1, source_target_pairs={{0,1},{1,0},{2,3},{3,2},{4,5},{5,4},{6,7},{7,6},{8,9},{9,8},{10,11... | collective-permute-start | bytes 393224 | tf_op jit(solution)/shard_map/ppermute | solution.py:425
  24.0 34.5 %copy-start = (bf16[2048,128]{1,0:T(8,128)(2,1)S(1)}, bf16[2048,128]{1,0:T(8,128)(2,1)}, u32[]{:S(2)}) copy-start(bf16[2048,128]{1,0:T(8,128)(2,1)} %head_ref.1) | copy-start | bytes 1572868
  24.0 34.5 %copy-start.1 = (bf16[1,1024,128]{2,1,0:T(8,128)(2,1)S(1)}, bf16[1,1024,128]{2,1,0:T(8,128)(2,1)}, u32[]{:S(2)}) copy-start(bf16[1,1024,128]{2,1,0:T(8,128)(2,1)} %param.14) | copy-start | bytes 786436
  24.0 34.5 %copy-start.2 = (f32[2048]{0:T(1024)S(1)}, f32[2048]{0:T(1024)}, u32[]{:S(2)}) copy-start(f32[2048]{0:T(1024)} %param.17) | copy-start | bytes 24580
  24.0 34.5 %copy-start.3 = (s32[1,8]{1,0:T(1,128)S(1)}, s32[1,8]{1,0:T(1,128)}, u32[]{:S(2)}) copy-start(s32[1,8]{1,0:T(1,128)} %valid_ref.1) | copy-start | bytes 100
  24.0 34.5 %copy-start.4 = (s32[128]{0:T(128)S(1)}, s32[128]{0:T(128)}, u32[]{:S(2)}) copy-start(s32[128]{0:T(128)} %param.21) | copy-start | bytes 1540
  36.9 16.8 %all-to-all-start.1 = ((bf16[16,64,128]{2,1,0:T(8,128)(2,1)}), bf16[16,64,128]{2,1,0:T(8,128)(2,1)S(1)}, u32[]{:S(2)}, u32[]{:S(2)}) async-start(bf16[16,64,128]{2,1,0:T(8,128)(2,1)} %scan_chips.1), calls=%async_computation.1 | async-start | bytes 524288 | tf_op jit(solution)/shard_map/all_to_all | solution.py:435
  43.8 13.7 %collective-permute-start.5 = (bf16[2,32,16,128]{3,2,1,0:T(8,128)(2,1)S(1)}, bf16[2,32,16,128]{3,2,1,0:T(8,128)(2,1)S(1)}, u32[]{:S(2)}, u32[]{:S(2)}) collective-permute-start(bf16[2,32,16,128]{3,2,1,0:T(8,128)(2,1)S(1)} %pad_maximum_fusion.q0_ref), channel_id=1, source_target_pairs={{0,6},{2,4},{4,2},{6,0},{1,7},{3,5},{5,3},{7,1},{8,14},{10,12},{12... | collective-permute-start | bytes 786440 | tf_op jit(solution)/shard_map/ppermute | solution.py:437
  46.4 11.1 %collective-permute-start.4 = (bf16[2,32,16,128]{3,2,1,0:T(8,128)(2,1)S(1)}, bf16[2,32,16,128]{3,2,1,0:T(8,128)(2,1)S(1)}, u32[]{:S(2)}, u32[]{:S(2)}) collective-permute-start(bf16[2,32,16,128]{3,2,1,0:T(8,128)(2,1)S(1)} %pad_maximum_fusion.q0_ref), channel_id=1, source_target_pairs={{0,4},{2,6},{4,0},{6,2},{1,5},{3,7},{5,1},{7,3},{8,12},{10,14},{12... | collective-permute-start | bytes 786440 | tf_op jit(solution)/shard_map/ppermute | solution.py:437
  46.9 10.6 %collective-permute-start.3 = (bf16[2,32,16,128]{3,2,1,0:T(8,128)(2,1)S(1)}, bf16[2,32,16,128]{3,2,1,0:T(8,128)(2,1)S(1)}, u32[]{:S(2)}, u32[]{:S(2)}) collective-permute-start(bf16[2,32,16,128]{3,2,1,0:T(8,128)(2,1)S(1)} %pad_maximum_fusion.q0_ref), channel_id=1, source_target_pairs={{0,2},{2,0},{4,6},{6,4},{1,3},{3,1},{5,7},{7,5},{8,10},{10,8},{12,... | collective-permute-start | bytes 786440 | tf_op jit(solution)/shard_map/ppermute | solution.py:437
  53.8 4.7 %collective-permute-start.2 = (bf16[16,64,128]{2,1,0:T(8,128)(2,1)S(1)}, bf16[16,64,128]{2,1,0:T(8,128)(2,1)S(1)}, u32[]{:S(2)}, u32[]{:S(2)}) collective-permute-start(bf16[16,64,128]{2,1,0:T(8,128)(2,1)S(1)} %get-tuple-element.43), channel_id=1, source_target_pairs={{0,8},{8,0},{1,9},{9,1},{2,10},{10,2},{3,11},{11,3},{4,12},{12,4},... | collective-permute-start | bytes 786440 | tf_op jit(solution)/shard_map/ppermute | solution.py:394
  58.5 1.0 copy-start.5

commit v3 on v1

--- a/solution.py
+++ b/solution.py
@@ -122,7 +122,7 @@
 
 
 def local_kernel(
-    dec_ref, b_ref, c_ref, x_ref, skip_ref, y_ref, g_ref,
+    first_head, dec_ref, b_ref, c_ref, x_ref, skip_ref, y_ref, g_ref,
     carry_ref, e_ref, cum_ref, rows_ref, factor_ref
 ):
     step = pl.program_id(0)
@@ -131,7 +131,7 @@
     @pl.when(step == 0)
     def _():
         carry_ref[...] = jnp.zeros_like(carry_ref)
-        e_ref[...] = head_selector(2 * HEADS, 0, INNER)
+        e_ref[...] = head_selector(2 * HEADS, first_head, INNER // 2)
         until = ones_where(col <= row)
         after = ones_where(col > row)
         sums_of = jnp.concatenate([until, after, jnp.ones((16, SPAN), BF16)], axis=0)
@@ -158,7 +158,7 @@
         c_span, b_span = c_ref[here, :], b_ref[here, :]
         b_turned = b_span.T
         cross = jnp.where(col <= row, dot_nt(c_span, b_span), 0.0)
-        for j in range(CHUNKS):
+        for j in range(CHUNKS // 2):
             wide = slice(j * WIDE, (j + 1) * WIDE)
             spread_out = dot(factors, e_ref[:, wide])
             carry = carry_ref[:, wide]
@@ -167,7 +167,7 @@
             parts = []
             for k in range(WIDE // 128):
                 mixes = []
-                for h in (j * 8 + 2 * k, j * 8 + 2 * k + 1):
+                for h in (first_head + j * 8 + 2 * k, first_head + j * 8 + 2 * k + 1):
                     spread = jnp.minimum(cum[:, h : h + 1] - cum_rows[h : h + 1, :], 0.0)
                     mixes.append((jnp.exp2(spread) * cross).astype(BF16))
                 x_pair = x_ref[here, j * WIDE + k * 128 : j * WIDE + (k + 1) * 128]
@@ -192,7 +192,7 @@
 
 
 def score_kernel(
-    base_ref, valid_ref, keep_ref, got_ref, c_ref, g_ref, y_any, z_any, gain_ref, head_ref,
+    base_ref, valid_ref, keep_ref, got_ref, c_ref, g_ref, left_any, right_any, z_any, gain_ref, head_ref,
     q0_ref, q1_ref, q2_ref, q3_ref, pair_ref, score_ref, paired_ref,
     e_ref, mean_ref, best_ref, enter_ref, q_ref, y_ref, z_ref, sems
 ):
@@ -201,7 +201,8 @@
     def fetches(i):
         rows = pl.ds(i * BLOCK, BLOCK)
         return (
-            pltpu.make_async_copy(y_any.at[rows, :], y_ref.at[i], sems.at[0, i]),
+            pltpu.make_async_copy(left_any.at[rows, :], y_ref.at[0, i], sems.at[0, i]),
+            pltpu.make_async_copy(right_any.at[rows, :], y_ref.at[1, i], sems.at[2, i]),
             pltpu.make_async_copy(z_any.at[rows, :], z_ref.at[i], sems.at[1, i]),
         )
 
@@ -231,7 +232,7 @@
     embedded = jnp.zeros((BLOCK, EMB), F32)
     for j in range(2):
         wide = slice(j * INNER // 2, (j + 1) * INNER // 2)
-        y = y_ref[step, :, wide].astype(F32) + dot(factors, e_ref[:, wide]) * dot(c_part, enter_ref[:, wide])
+        y = y_ref[j, step].astype(F32) + dot(factors, e_ref[:, wide]) * dot(c_part, enter_ref[:, wide])
         z_half = 0.5 * z_ref[step, :, wide].astype(F32)
         gated = y * (z_half + z_half * jnp.tanh(z_half))
         squares = (gated * gated).astype(BF16)
@@ -302,34 +303,36 @@
     )(core, decays, b, x)
 
 
-def local_part(decays, b, c, x, skip):
-    def tokens(columns):
-        return pl.BlockSpec((TOGETHER * SPAN, columns), lambda i: (i, 0))
+def local_part(half, decays, b, c, x, skip):
+    width = INNER // 2
+
+    def tokens(columns, place=0):
+        return pl.BlockSpec((TOGETHER * SPAN, columns), lambda i: (i, place))
 
     return pl.pallas_call(
-        local_kernel,
+        functools.partial(local_kernel, half * (HEADS // 2)),
         grid=(SPANS // TOGETHER,),
         in_specs=[
             whole((HEADS, TOKENS)),
             tokens(STATE),
             tokens(STATE),
-            tokens(INNER),
-            whole((1, INNER)),
-        ],
-        out_specs=[tokens(INNER), whole((TOKENS, 2 * HEADS))],
+            tokens(width, half),
+            pl.BlockSpec((1, width), lambda i: (0, half)),
+        ],
+        out_specs=[tokens(width), whole((TOKENS, 2 * HEADS))],
         out_shape=[
-            jax.ShapeDtypeStruct((TOKENS, INNER), BF16),
+            jax.ShapeDtypeStruct((TOKENS, width), BF16),
             jax.ShapeDtypeStruct((TOKENS, 2 * HEADS), BF16),
         ],
         scratch_shapes=[
-            pltpu.VMEM((STATE, INNER), F32),
-            pltpu.VMEM((2 * HEADS, INNER), BF16),
+            pltpu.VMEM((STATE, width), F32),
+            pltpu.VMEM((2 * HEADS, width), BF16),
             pltpu.VMEM((SPANS, SPAN, HEADS), F32),
             pltpu.VMEM((SPANS, HEADS, SPAN), F32),
             pltpu.VMEM((SPANS, 2 * SPAN + 16, 2 * HEADS), BF16),
         ],
         compiler_params=params(60),
-        cost_estimate=cost(8 * 10**9, 9 * 10**6, 4 * 10**6),
+        cost_estimate=cost(4 * 10**9, 5 * 10**6, 2 * 10**6),
         name="local_part",
     )(decays, b, c, x, skip)
 
@@ -344,7 +347,7 @@
     )(states)
 
 
-def scores(base, valid_len, keep, got, c, growth, y, z, gain, w_head, q, pair_ids):
+def scores(base, valid_len, keep, got, c, growth, left, right, z, gain, w_head, q, pair_ids):
     def tokens(width):
         return pl.BlockSpec((BLOCK, width), lambda i: (i, 0))
 
@@ -364,6 +367,7 @@
             tokens(2 * HEADS),
             far,
             far,
+            far,
             whole((1, INNER)),
             whole((INNER, EMB)),
             *[whole((2, QTOK, QTOT // 8, EMB))] * 4,
@@ -380,14 +384,14 @@
             pltpu.VMEM((SPANS, QTOK * QTOT), F32),
             pltpu.VMEM((STATE, INNER), BF16),
             pltpu.VMEM((QTOK * QTOT, EMB), BF16),
+            pltpu.VMEM((2, TOKENS // BLOCK, BLOCK, INNER // 2), BF16),
             pltpu.VMEM((TOKENS // BLOCK, BLOCK, INNER), BF16),
-            pltpu.VMEM((TOKENS // BLOCK, BLOCK, INNER), BF16),
-            pltpu.SemaphoreType.DMA((2, TOKENS // BLOCK)),
+            pltpu.SemaphoreType.DMA((3, TOKENS // BLOCK)),
         ],
         compiler_params=params(60),
         cost_estimate=cost(6 * 10**9, 11 * 10**6, 2 * 10**6),
         name="scores",
-    )(base, valid_len, keep, got, c, growth, y, z, gain, w_head, *q, pair_ids)
+    )(base, valid_len, keep, got, c, growth, left, right, z, gain, w_head, *q, pair_ids)
 
 
 def swap_cores(v):
@@ -425,15 +429,17 @@
     place = lax.axis_index(("z", "y_lo", "core"))
     base = jnp.stack([(document * 32 + place) * SPANS, core, document])
     skip = jnp.repeat(d_skip, HEAD_DIM).reshape(1, INNER)
-    y, growth = local_part(decay, b, c, x, skip)
-    by_pair, y, growth, q_pair, base = lax.optimization_barrier(
-        (by_pair, y, growth, q_pair, base)
+    left, growth = local_part(0, decay, b, c, x, skip)
+    by_pair, left, growth, q_pair, base = lax.optimization_barrier(
+        (by_pair, left, growth, q_pair, base)
     )
-    prefix, q_pair = lax.optimization_barrier((scan_chips(by_pair), q_pair))
+    prefix, q_pair, decay = lax.optimization_barrier((scan_chips(by_pair), q_pair, decay))
     entering = lax.all_to_all(prefix, ("z", "y_lo"), 0, 0, tiled=True)
     q_parts = [q_pair] + [
         lax.ppermute(q_pair, "x", [(i, i ^ d) for i in range(4)]) for d in range(1, 4)
     ]
+    right, _ = local_part(1, decay, b, c, x, skip)
+    entering, right = lax.optimization_barrier((entering, right))
     after = (
         d_first * entering.astype(F32) + first[:, :HALF].astype(F32)
     ).astype(BF16)
@@ -441,8 +447,8 @@
     got = swap_cores(jnp.where(lower, after, entering))
 
     maxsim, paired = scores(
-        base, valid_len, keep, got, c, growth, y, z, norm_gain.reshape(1, INNER), w_head, q_parts,
-        pair_ids.reshape(1, QTOT),
+        base, valid_len, keep, got, c, growth, left, right, z, norm_gain.reshape(1, INNER), w_head,
+        q_parts, pair_ids.reshape(1, QTOT),
     )
     everything = lax.all_to_all(paired, ("z", "y_lo", "core", "x", "y_hi"), 0, 0, tiled=True)
     return maxsim[None], jnp.sum(everything, axis=0)

time: 99.7 us -> 96.2 us (0.965)
  waiting for transfers between devices: 7.71 us -> 4.19 us
  Pallas kernels: 32.1 us -> 35.5 us
  starting transfers between devices: 27.2 us -> 25.1 us
  blocking collectives: 25.4 us -> 23.9 us
    all_to_all x1, waiting for transfers between devices: 6.5 us -> 0.01 us  [on_device(): entering = lax.all_to_all(prefix, ('z', 'y_lo'), 0, 0, tiled=True)]
    pallas_call x1 -> x2, Pallas kernels: 11.9 us -> 15.3 us  [local_part(): pl.pallas_call(functools.partial(local_kernel, half * (HEADS // 2)), grid...]
    ppermute x3, waiting for transfers between devices: 0.01 us -> 2.33 us  [on_device(): lax.ppermute(q_pair, 'x', [(i, i ^ d) for i in range(4)])]
    all_to_all x1, waiting for transfers between devices: 0.01 us -> 1.83 us  [on_device(): by_pair = lax.all_to_all(packed, ('z', 'y_lo'), 0, 0, tiled=True)]
    all_to_all x1, starting transfers between devices: 6.95 us -> 5.16 us  [on_device(): entering = lax.all_to_all(prefix, ('z', 'y_lo'), 0, 0, tiled=True)]
    all_to_all x1, blocking collectives: 25.4 us -> 23.9 us  [on_device(): lax.all_to_all(paired, ('z', 'y_lo', 'core', 'x', 'y_hi'), 0, 0, tiled=True)]
    ppermute x2, waiting for transfers between devices: 1.2 us -> 0.03 us  [swap_cores(): return lax.ppermute(v, 'core', [(0, 1), (1, 0)])]
  transfers between devices with their start and end apart: 8 -> 8, of which waited for: 3 -> 2; matrix products, arithmetic and copies ran while one was open for 3% -> 3% of each run, Pallas kernels for 12% -> 16%
where the time goes in v3:
time: 96.2 us; the launch traced here: 95.6 us
  Pallas kernels  35.5 us (37%)
  starting transfers between devices  25.1 us (26%)
  blocking collectives  23.9 us (25%)
  other arithmetic  4.56 us (5%)
  waiting for transfers between devices  4.19 us (4%)
  local copies, waits for them, and re-layouts  1.65 us (2%)
    all_to_all x1, blocking collectives, on_device(): lax.all_to_all(paired, ('z', 'y_lo', 'core', 'x', 'y_hi'), 0, 0, tiled=True)  23.9 us
    pallas_call x2, Pallas kernels, local_part(): pl.pallas_call(functools.partial(local_kernel, half * (HEADS // 2)), grid...  15.3 us
    pallas_call x1, Pallas kernels, scores(): pl.pallas_call(score_kernel, grid=(TOKENS // BLOCK,), in_specs=[smem, sme...  14.3 us
    all_to_all x1, starting transfers between devices, on_device(): by_pair = lax.all_to_all(packed, ('z', 'y_lo'), 0, 0, tiled=True)  7.58 us
    ppermute x2, starting transfers between devices, swap_cores(): return lax.ppermute(v, 'core', [(0, 1), (1, 0)])  5.66 us
    pallas_call x1, Pallas kernels, device_states(): pl.pallas_call(states_kernel, in_specs=[pl.BlockSpec(memory_space=pltpu.S...  5.18 us
    all_to_all x1, starting transfers between devices, on_device(): entering = lax.all_to_all(prefix, ('z', 'y_lo'), 0, 0, tiled=True)  5.16 us
    ppermute x3, starting transfers between devices, on_device(): lax.ppermute(q_pair, 'x', [(i, i ^ d) for i in range(4)])  3.95 us
  transfers between devices with their start and end apart: 8, of which 2 were waited for; matrix products, arithmetic and copies ran while one was open for 3% of the time, Pallas kernels for 16%

profile of v3, /device:TPU:1, one launch (start us, length us, event | category | flops | bytes accessed | tf_op | source)
XLA Modules:
  0.0 95.6 jit_solution(1851573196856957202)
XLA Ops:
  0.7 5.2 %device_states.1 = (bf16[16,80,128]{2,1,0:T(8,128)(2,1)}, bf16[16,80,128]{2,1,0:T(8,128)(2,1)}) custom-call(s32[1]{0:T(128)} %bitcast.core_ref, f32[32,1024]{1,0:T(8,128)} %bitcast.27, bf16[1024,128]{1,0:T(8,128)(2,1)} %bitcast.24, bf16[1024,2048]{1,0:T(8,128)(2,1)} %bitcast.20), custom_call_target="tpu_custom_call" | custom-call | flops 1000000000 | bytes 5000000 | tf_op jit(solution)/shard_map/device_states/pallas_call | solution.py:287
  5.8 3.3 %collective-permute-start = (bf16[16,80,128]{2,1,0:T(8,128)(2,1)}, bf16[16,80,128]{2,1,0:T(8,128)(2,1)S(1)}, u32[]{:S(2)}, u32[]{:S(2)}) collective-permute-start(bf16[16,80,128]{2,1,0:T(8,128)(2,1)} %get-tuple-element.22), channel_id=1, source_target_pairs={{0,8},{8,0},{1,9},{9,1},{2,10},{10,2},{3,11},{11,3},{4,12},{12,4},... | collective-permute-start | bytes 983048 | tf_op jit(solution)/shard_map/ppermute | solution.py:398
  9.2 0.1 broadcast_in_dim.11
  9.2 0.7 reshape_reshape.3.skip_ref
  9.9 0.1 pad.8.clone
  10.0 0.6 pad_add_fusion.base_ref
  10.6 0.0 collective-permute-done
  10.6 1.0 %broadcast_select_fusion = (bf16[16,80,128]{2,1,0:T(8,128)(2,1)S(1)}, bf16[16,80,128]{2,1,0:T(8,128)(2,1)S(1)}) fusion(bf16[16,80,128]{2,1,0:T(8,128)(2,1)} %get-tuple-element.23, bf16[16,80,128]{2,1,0:T(8,128)(2,1)S(1)} %collective-permute-done, pred[]{:T(512)S(6)} %eq.3), kind=kLoop, calls=%fused_computation.10 | loop fusion | flops 327680 | bytes 1310721 | tf_op jit(solution)/shard_map/jit(_where)/select_n | solution.py:414
  11.7 0.1 fusion.1
  11.8 0.9 maximum_maximum_fusion
  12.7 0.1 fusion.5
  12.8 7.6 %all-to-all-start = ((bf16[16,80,128]{2,1,0:T(8,128)(2,1)}), bf16[16,80,128]{2,1,0:T(8,128)(2,1)S(1)}, u32[]{:S(2)}, u32[]{:S(2)}) async-start(bf16[16,80,128]{2,1,0:T(8,128)(2,1)} %maximum_maximum_fusion), calls=%async_computation | async-start | bytes 655360 | tf_op jit(solution)/shard_map/all_to_all | solution.py:422
  20.4 0.1 fusion.7
  20.6 2.7 %collective-permute-start.1 = (bf16[32,16,128]{2,1,0:T(8,128)(2,1)S(1)}, bf16[32,16,128]{2,1,0:T(8,128)(2,1)S(1)}, u32[]{:S(2)}, u32[]{:S(2)}) collective-permute-start(bf16[32,16,128]{2,1,0:T(8,128)(2,1)S(1)} %fusion.7), channel_id=1, source_target_pairs={{0,1},{1,0},{2,3},{3,2},{4,5},{5,4},{6,7},{7,6},{8,9},{9,8},{10,11... | collective-permute-start | bytes 393224 | tf_op jit(solution)/shard_map/ppermute | solution.py:427
  23.3 7.6 %local_part.2 = (bf16[1024,1024]{1,0:T(8,128)(2,1)}, bf16[1024,64]{1,0:T(8,128)(2,1)}) custom-call(f32[32,1024]{1,0:T(8,128)} %bitcast.28, bf16[1024,128]{1,0:T(8,128)(2,1)} %bitcast.25, bf16[1024,128]{1,0:T(8,128)(2,1)} %bitcast.35, bf16[1024,2048]{1,0:T(8,128)(2,1)} %bitcast.21, f32[1,2048]{1,0:T(1,128)} %reshape_reshape.3.skip_ref), custom_call_target="tpu_custom_call" | custom-call | flops 4000000000 | bytes 5000000 | tf_op jit(solution)/shard_map/local_part/pallas_call | solution.py:312
  31.0 1.8 %all-to-all-done.in_ref = bf16[16,80,128]{2,1,0:T(8,128)(2,1)S(1)} async-done(((bf16[16,80,128]{2,1,0:T(8,128)(2,1)}), bf16[16,80,128]{2,1,0:T(8,128)(2,1)S(1)}, u32[]{:S(2)}, u32[]{:S(2)}) %all-to-all-start) | async-done | bytes 327712 | tf_op jit(solution)/shard_map/all_to_all | solution.py:422
  32.8 0.8 scan_chips.1
  33.6 5.2 %all-to-all-start.1 = ((bf16[16,64,128]{2,1,0:T(8,128)(2,1)}), bf16[16,64,128]{2,1,0:T(8,128)(2,1)S(1)}, u32[]{:S(2)}, u32[]{:S(2)}) async-start(bf16[16,64,128]{2,1,0:T(8,128)(2,1)} %scan_chips.1), calls=%async_computation.1 | async-start | bytes 524288 | tf_op jit(solution)/shard_map/all_to_all | solution.py:437
  38.7 1.3 %collective-permute-start.3 = (bf16[2,32,16,128]{3,2,1,0:T(8,128)(2,1)S(1)}, bf16[2,32,16,128]{3,2,1,0:T(8,128)(2,1)S(1)}, u32[]{:S(2)}, u32[]{:S(2)}) collective-permute-start(bf16[2,32,16,128]{3,2,1,0:T(8,128)(2,1)S(1)} %pad_maximum_fusion.q0_ref), channel_id=1, source_target_pairs={{0,2},{2,0},{4,6},{6,4},{1,3},{3,1},{5,7},{7,5},{8,10},{10,8},{12,... | collective-permute-start | bytes 786440 | tf_op jit(solution)/shard_map/ppermute | solution.py:439
  40.0 2.4 %collective-permute-start.4 = (bf16[2,32,16,128]{3,2,1,0:T(8,128)(2,1)S(1)}, bf16[2,32,16,128]{3,2,1,0:T(8,128)(2,1)S(1)}, u32[]{:S(2)}, u32[]{:S(2)}) collective-permute-start(bf16[2,32,16,128]{3,2,1,0:T(8,128)(2,1)S(1)} %pad_maximum_fusion.q0_ref), channel_id=1, source_target_pairs={{0,4},{2,6},{4,0},{6,2},{1,5},{3,7},{5,1},{7,3},{8,12},{10,14},{12... | collective-permute-start | bytes 786440 | tf_op jit(solution)/shard_map/ppermute | solution.py:439
  42.5 0.2 collective-permute-start.5
  42.7 7.6 %local_part.3 = (bf16[1024,1024]{1,0:T(8,128)(2,1)}, bf16[1024,64]{1,0:T(8,128)(2,1)}) custom-call(f32[32,1024]{1,0:T(8,128)} %bitcast.29, bf16[1024,128]{1,0:T(8,128)(2,1)} %bitcast.26, bf16[1024,128]{1,0:T(8,128)(2,1)} %bitcast.36, bf16[1024,2048]{1,0:T(8,128)(2,1)} %bitcast.22, f32[1,2048]{1,0:T(1,128)} %reshape_reshape.3.skip_ref), custom_call_target="tpu_custom_call" | custom-call | flops 4000000000 | bytes 5000000 | tf_op jit(solution)/shard_map/local_part/pallas_call | solution.py:312
  50.3 0.8 fusion.3
  51.2 2.3 %collective-permute-start.2 = (bf16[16,64,128]{2,1,0:T(8,128)(2,1)S(1)}, bf16[16,64,128]{2,1,0:T(8,128)(2,1)S(1)}, u32[]{:S(2)}, u32[]{:S(2)}) collective-permute-start(bf16[16,64,128]{2,1,0:T(8,128)(2,1)S(1)} %get-tuple-element.47), channel_id=1, source_target_pairs={{0,8},{8,0},{1,9},{9,1},{2,10},{10,2},{3,11},{11,3},{4,12},{12,4},... | collective-permute-start | bytes 786440 | tf_op jit(solution)/shard_map/ppermute | solution.py:398
  53.5 0.0 collective-permute-done.4.q2_ref
  53.5 2.3 %collective-permute-done.5.q3_ref = bf16[2,32,16,128]{3,2,1,0:T(8,128)(2,1)S(1)} collective-permute-done((bf16[2,32,16,128]{3,2,1,0:T(8,128)(2,1)S(1)}, bf16[2,32,16,128]{3,2,1,0:T(8,128)(2,1)S(1)}, u32[]{:S(2)}, u32[]{:S(2)}) %collective-permute-start.5) | collective-permute-done | bytes 262176 | tf_op jit(solution)/shard_map/ppermute | solution.py:439
  55.8 0.0 collective-permute-done.2.got_ref
  55.9 0.7 copy-done.5
  56.6 0.1 copy-done.6
  56.7 14.3 %scores.1 = (f32[8,128]{1,0:T(8,128)}, f32[256,128]{1,0:T(8,128)}) custom-call(s32[3]{0:T(128)} %pad_add_fusion.base_ref, s32[1,8]{1,0:T(1,128)} %valid_ref.1, bf16[16,64,128]{2,1,0:T(8,128)(2,1)} %get-tuple-element.48.keep_ref, bf16[16,64,128]{2,1,0:T(8,128)(2,1)} %copy-done.6, bf16[1024,128]{1,0:T(8,128)(2,1)} %bitcast.37, ...), custom_call_target="tpu_custom_call" | custom-call | flops 6000000000 | bytes 11000000 | tf_op jit(solution)/shard_map/scores/pallas_call | solution.py:358
  71.0 23.9 %all_to_all.19 = f32[256,1,128]{2,1,0:T(1,128)S(1)} all-to-all(f32[256,1,128]{2,1,0:T(1,128)} %bitcast.30), channel_id=1, replica_groups=mesh['z'=8,'y_lo'=2,'core'=2,'x'=4,'y_hi'=2] {'z','y_lo','core','x','y_hi'}, dimensions={0} | all-to-all | bytes 262144 | tf_op jit(solution)/shard_map/all_to_all | solution.py:453
  94.8 0.8 reduce_sum.19
  (20 shorter events, 0.1 us)
Async XLA Ops:
  0.6 8.5 %copy-start.2 = (f32[32]{0:T(128)S(1)}, f32[32]{0:T(128)}, u32[]{:S(2)}) copy-start(f32[32]{0:T(128)} %param.16) | copy-start | bytes 388
  0.6 12.0 %copy-start = (bf16[16,32,128]{2,1,0:T(8,128)(2,1)S(1)}, bf16[16,32,128]{2,1,0:T(8,128)(2,1)}, u32[]{:S(2)}) copy-start(bf16[16,32,128]{2,1,0:T(8,128)(2,1)} %param.19) | copy-start | bytes 393220
  5.8 4.8 %collective-permute-start = (bf16[16,80,128]{2,1,0:T(8,128)(2,1)}, bf16[16,80,128]{2,1,0:T(8,128)(2,1)S(1)}, u32[]{:S(2)}, u32[]{:S(2)}) collective-permute-start(bf16[16,80,128]{2,1,0:T(8,128)(2,1)} %get-tuple-element.22), channel_id=1, source_target_pairs={{0,8},{8,0},{1,9},{9,1},{2,10},{10,2},{3,11},{11,3},{4,12},{12,4},... | collective-permute-start | bytes 983048 | tf_op jit(solution)/shard_map/ppermute | solution.py:398
  12.8 19.9 %all-to-all-start = ((bf16[16,80,128]{2,1,0:T(8,128)(2,1)}), bf16[16,80,128]{2,1,0:T(8,128)(2,1)S(1)}, u32[]{:S(2)}, u32[]{:S(2)}) async-start(bf16[16,80,128]{2,1,0:T(8,128)(2,1)} %maximum_maximum_fusion), calls=%async_computation | async-start | bytes 655360 | tf_op jit(solution)/shard_map/all_to_all | solution.py:422
  20.6 10.3 %collective-permute-start.1 = (bf16[32,16,128]{2,1,0:T(8,128)(2,1)S(1)}, bf16[32,16,128]{2,1,0:T(8,128)(2,1)S(1)}, u32[]{:S(2)}, u32[]{:S(2)}) collective-permute-start(bf16[32,16,128]{2,1,0:T(8,128)(2,1)S(1)} %fusion.7), channel_id=1, source_target_pairs={{0,1},{1,0},{2,3},{3,2},{4,5},{5,4},{6,7},{7,6},{8,9},{9,8},{10,11... | collective-permute-start | bytes 393224 | tf_op jit(solution)/shard_map/ppermute | solution.py:427
  30.9 19.4 %copy-start.1 = (bf16[2,32,16,128]{3,2,1,0:T(8,128)(2,1)}, bf16[2,32,16,128]{3,2,1,0:T(8,128)(2,1)S(1)}, u32[]{:S(2)}) copy-start(bf16[2,32,16,128]{3,2,1,0:T(8,128)(2,1)S(1)} %pad_maximum_fusion.q0_ref) | copy-start | bytes 786436
  33.6 16.8 %all-to-all-start.1 = ((bf16[16,64,128]{2,1,0:T(8,128)(2,1)}), bf16[16,64,128]{2,1,0:T(8,128)(2,1)S(1)}, u32[]{:S(2)}, u32[]{:S(2)}) async-start(bf16[16,64,128]{2,1,0:T(8,128)(2,1)} %scan_chips.1), calls=%async_computation.1 | async-start | bytes 524288 | tf_op jit(solution)/shard_map/all_to_all | solution.py:437
  38.7 14.8 %collective-permute-start.3 = (bf16[2,32,16,128]{3,2,1,0:T(8,128)(2,1)S(1)}, bf16[2,32,16,128]{3,2,1,0:T(8,128)(2,1)S(1)}, u32[]{:S(2)}, u32[]{:S(2)}) collective-permute-start(bf16[2,32,16,128]{3,2,1,0:T(8,128)(2,1)S(1)} %pad_maximum_fusion.q0_ref), channel_id=1, source_target_pairs={{0,2},{2,0},{4,6},{6,4},{1,3},{3,1},{5,7},{7,5},{8,10},{10,8},{12,... | collective-permute-start | bytes 786440 | tf_op jit(solution)/shard_map/ppermute | solution.py:439
  40.0 13.5 %collective-permute-start.4 = (bf16[2,32,16,128]{3,2,1,0:T(8,128)(2,1)S(1)}, bf16[2,32,16,128]{3,2,1,0:T(8,128)(2,1)S(1)}, u32[]{:S(2)}, u32[]{:S(2)}) collective-permute-start(bf16[2,32,16,128]{3,2,1,0:T(8,128)(2,1)S(1)} %pad_maximum_fusion.q0_ref), channel_id=1, source_target_pairs={{0,4},{2,6},{4,0},{6,2},{1,5},{3,7},{5,1},{7,3},{8,12},{10,14},{12... | collective-permute-start | bytes 786440 | tf_op jit(solution)/shard_map/ppermute | solution.py:439
  42.5 13.4 %collective-permute-start.5 = (bf16[2,32,16,128]{3,2,1,0:T(8,128)(2,1)S(1)}, bf16[2,32,16,128]{3,2,1,0:T(8,128)(2,1)S(1)}, u32[]{:S(2)}, u32[]{:S(2)}) collective-permute-start(bf16[2,32,16,128]{3,2,1,0:T(8,128)(2,1)S(1)} %pad_maximum_fusion.q0_ref), channel_id=1, source_target_pairs={{0,6},{2,4},{4,2},{6,0},{1,7},{3,5},{5,3},{7,1},{8,14},{10,12},{12... | collective-permute-start | bytes 786440 | tf_op jit(solution)/shard_map/ppermute | solution.py:439
  51.2 4.7 %collective-permute-start.2 = (bf16[16,64,128]{2,1,0:T(8,128)(2,1)S(1)}, bf16[16,64,128]{2,1,0:T(8,128)(2,1)S(1)}, u32[]{:S(2)}, u32[]{:S(2)}) collective-permute-start(bf16[16,64,128]{2,1,0:T(8,128)(2,1)S(1)} %get-tuple-element.47), channel_id=1, source_target_pairs={{0,8},{8,0},{1,9},{9,1},{2,10},{10,2},{3,11},{11,3},{4,12},{12,4},... | collective-permute-start | bytes 786440 | tf_op jit(solution)/shard_map/ppermute | solution.py:398
  53.5 2.3 %copy-start.3 = (bf16[2,32,16,128]{3,2,1,0:T(8,128)(2,1)}, bf16[2,32,16,128]{3,2,1,0:T(8,128)(2,1)S(1)}, u32[]{:S(2)}) copy-start(bf16[2,32,16,128]{3,2,1,0:T(8,128)(2,1)S(1)} %collective-permute-done.3.q1_ref) | copy-start | bytes 786436
  53.5 2.3 %copy-start.4 = (bf16[2,32,16,128]{3,2,1,0:T(8,128)(2,1)}, bf16[2,32,16,128]{3,2,1,0:T(8,128)(2,1)S(1)}, u32[]{:S(2)}) copy-start(bf16[2,32,16,128]{3,2,1,0:T(8,128)(2,1)S(1)} %collective-permute-done.4.q2_ref) | copy-start | bytes 786436
  55.8 0.7 copy-start.5
  55.8 0.8 copy-start.6
